TPU v7x, 128 devices: a whole 4x4x4 slice. The times are simulated.
128 devices in a mesh: layer: 4 (over y), grid: 32 (over x, z, core).
Axes of the slice: x: 4, y: 4, z: 4, core: 2. Of those that a mesh axis runs over, the one named last changes fastest.
Arguments:
- leaf_inverse: float32 [4, 32, 4, 128, 128], P('layer', 'grid'), may hold values from -1 to 2
- leaf_coupling: float32 [4, 32, 4, 128, 128], P('layer', 'grid'), may hold values from -0.5 to 0.5
- leaf_rhs: float32 [4, 32, 4, 128, 128], P('layer', 'grid'), may hold values from -6 to 6
- mid_inverse: float32 [4, 32, 2, 128, 128], P('layer', 'grid'), may hold values from -1 to 2
- mid_coupling: float32 [4, 32, 2, 128, 128], P('layer', 'grid'), may hold values from -0.375 to 0.375
- mid_rhs: float32 [4, 32, 2, 128, 128], P('layer', 'grid'), may hold values from -6 to 6
- mid_top: float32 [4, 32, 2, 4096, 128], P('layer', 'grid'), may hold values from -0.0546875 to 0.0546875
- root_inverse: float32 [4, 32, 128, 128], P('layer', 'grid'), may hold values from -1 to 2
- root_top: float32 [4, 32, 4096, 128], P('layer', 'grid'), may hold values from -0.0546875 to 0.0546875
- root_rhs: float32 [4, 32, 128, 128], P('layer', 'grid'), may hold values from -6 to 6
- top_inverse: float32 [32, 128, 128], P('grid'), may hold values from -1 to 2
- top_factor: float32 [32, 128, 4096], P('grid'), may hold values from -0.25 to 0.25
- top_rhs: float32 [32, 128, 128], P('grid'), may hold values from -6 to 6
- top_pattern: int32 [32, 32], P('grid'), may hold values from 0 to 1, as said below
Outputs:
- leaf_solution: float32 [4, 32, 4, 128, 128], P('layer', 'grid')
- mid_solution: float32 [4, 32, 2, 128, 128], P('layer', 'grid')
- root_solution: float32 [4, 32, 128, 128], P('layer', 'grid')
- top_solution: float32 [32, 128, 128], P('grid')
Inputs may be any that keep to these rules, and one draw needn't show every extreme that they name: `top_pattern`: entries (i, j) with j // 4 >= i // 4 are not read; entry (i, 0) is 1 for every i >= 4.
All inputs are finite; a program needn't handle non-finite values.
Results may differ from a plain program's by a relative error of at most 0.00011.
Values sent between devices are 32-bit elements; how exact they have to be, the bound alone decides.
No kernel may reach another device: no remote copies, remote signals or barrier semaphores. Data moves between devices by JAX's collectives and lax.ppermute only.
A program may use at most 64 MiB of HBM per device.

v0:
```python
import jax
import jax.numpy as jnp
from jax import lax
from jax.sharding import PartitionSpec as P

SPAN = 4


def product(spec, left, right):
    return jnp.einsum(
        spec, left, right, precision=lax.Precision.HIGHEST, preferred_element_type=jnp.float32
    )


def transposed(left, right):
    return lax.dot_general(
        left,
        right,
        (((0,), (0,)), ((), ())),
        precision=lax.Precision.HIGHEST,
        preferred_element_type=jnp.float32,
    )


def pack_slot(value, slot, span):
    picks = (jnp.arange(span) == slot)[:, None, None]
    return jnp.where(picks, value[None], jnp.zeros((), jnp.float32))


def local(
    leaf_inverse,
    leaf_coupling,
    leaf_rhs,
    mid_inverse,
    mid_coupling,
    mid_rhs,
    mid_top,
    root_inverse,
    root_top,
    root_rhs,
    top_inverse,
    top_factor,
    top_rhs,
    top_pattern,
):
    block_width = leaf_inverse.shape[-1]
    columns = leaf_rhs.shape[-1]
    blocks_top = lax.axis_size("grid")
    position = lax.axis_index("grid")
    span = SPAN
    group_count = blocks_top // span
    own_group = position // span
    leaf_inv = leaf_inverse[0, 0]
    leaf_links = leaf_coupling[0, 0]
    forward_leaf = product("pab,pbr->par", leaf_inv, leaf_rhs[0, 0])
    pulled = (
        product("pab,pbr->par", leaf_links, forward_leaf)
        .reshape(-1, 2, block_width, columns)
        .sum(axis=1)
    )
    forward_mid = product("mab,mbr->mar", mid_inverse[0, 0], mid_rhs[0, 0] - pulled)
    root_input = root_rhs[0, 0] - product("mab,mbr->ar", mid_coupling[0, 0], forward_mid)
    forward_root = product("ab,br->ar", root_inverse[0, 0], root_input)
    root_panel = root_top[0, 0]
    mid_panel = mid_top[0, 0]
    root_rows = root_panel
    mid_rows = mid_panel
    summed = product("kb,br->kr", root_rows, forward_root) + product(
        "mkb,mbr->kr", mid_rows, forward_mid
    )
    partial_sums = lax.psum_scatter(
        summed.reshape(1 * lax.axis_size("grid"), block_width, columns),
        "grid",
        scatter_dimension=0,
        tiled=True,
    )
    reduced = lax.psum(partial_sums, "layer")
    residual = top_rhs[0] - reduced[0]
    top_inv = top_inverse[0]
    factor_row = top_factor[0]
    pattern_row = top_pattern[0]

    def weights_of(group):
        stored = lax.dynamic_slice_in_dim(pattern_row, group * span, span)
        return jnp.where(group < own_group, stored, 0).astype(jnp.float32)

    def panel_of(group):
        return lax.dynamic_slice_in_dim(
            factor_row, group * span * block_width, span * block_width, 1
        )

    def forward_step(group, carried):
        residual, solved_own = carried
        candidate = jnp.dot(
            top_inv, residual, precision=lax.Precision.HIGHEST, preferred_element_type=jnp.float32
        )
        slot = position - group * span
        solved = lax.psum(pack_slot(candidate, slot, span), "grid")
        scaled = (weights_of(group)[:, None, None] * solved).reshape(span * block_width, columns)
        update = jnp.dot(
            panel_of(group),
            scaled,
            precision=lax.Precision.HIGHEST,
            preferred_element_type=jnp.float32,
        )
        residual = residual - update
        solved_own = jnp.where(own_group == group, candidate, solved_own)
        return (residual, solved_own)

    residual, forward_top = lax.fori_loop(
        0, group_count, forward_step, (residual, jnp.zeros_like(residual))
    )

    def contribution(group, back_own):
        terms = transposed(panel_of(group), back_own).reshape(span, block_width, columns)
        return weights_of(group)[:, None, None] * terms

    def settle(group, pulled_group, back_own):
        slot = jnp.clip(position - group * span, 0, span - 1)
        pulled_top = lax.dynamic_index_in_dim(pulled_group, slot, 0, keepdims=False)
        candidate = transposed(top_inv, forward_top - pulled_top)
        return jnp.where(own_group == group, candidate, back_own)

    def back_step(sweep_step, back_own):
        group = group_count - 1 - sweep_step
        pulled_group = lax.psum(contribution(group, back_own), "grid")
        return settle(group, pulled_group, back_own)

    back_own = lax.fori_loop(0, group_count, back_step, jnp.zeros_like(forward_top))
    shard_piece = lax.all_gather(back_own[None], "grid", axis=0, tiled=True)
    amount = shard_piece.shape[0]
    flat_rows = shard_piece.reshape(amount * block_width, columns)
    root_rows = root_panel
    mid_rows = mid_panel
    root_pull = transposed(root_rows, flat_rows)
    mid_pull = product("mkb,kr->mbr", mid_rows, flat_rows)
    back_root = product("ba,br->ar", root_inverse[0, 0], forward_root - root_pull)
    back_mid = product(
        "mba,mbr->mar",
        mid_inverse[0, 0],
        forward_mid - product("mab,ar->mbr", mid_coupling[0, 0], back_root) - mid_pull,
    )
    parent = jnp.repeat(back_mid, 2, axis=0)
    back_leaf = product(
        "pba,pbr->par", leaf_inv, forward_leaf - product("pab,par->pbr", leaf_links, parent)
    )
    return (back_leaf[None, None], back_mid[None, None], back_root[None, None], back_own[None])


def solution(mesh):
    placed = (
        P("layer", "grid", None, None, None),
        P("layer", "grid", None, None, None),
        P("layer", "grid", None, None, None),
        P("layer", "grid", None, None, None),
        P("layer", "grid", None, None, None),
        P("layer", "grid", None, None, None),
        P("layer", "grid", None, None, None),
        P("layer", "grid", None, None),
        P("layer", "grid", None, None),
        P("layer", "grid", None, None),
        P("grid", None, None),
        P("grid", None, None),
        P("grid", None, None),
        P("grid", None),
    )
    return jax.shard_map(
        local,
        mesh=mesh,
        in_specs=placed,
        out_specs=(
            P("layer", "grid", None, None, None),
            P("layer", "grid", None, None, None),
            P("layer", "grid", None, None),
            P("grid", None, None),
        ),
        check_vma=False,
    )
```

profile of v0, /device:TPU:1, one launch (start us, length us, event | category | flops | bytes accessed | tf_op | source)
XLA Modules:
  0.0 1938.6 jit_solution(1425876203916425412)
XLA Ops:
  9.8 1.6 bitcast_reduce_fusion
  12.7 6.5 convolution_bitcast_fusion.1
  19.8 3.4 fusion.14
  23.2 2.9 copy.38
  26.2 80.7 %reduce-scatter.2.cloned.1.call-done = f32[1,128,128]{2,1,0:T(8,128)} async-done(((f32[32,128,128]{2,1,0:T(8,128)}), f32[1,128,128]{2,1,0:T(8,128)}) %reduce-scatter.2.cloned.1.call-update) | async-done | bytes 65552 | tf_op jit(solution)/shard_map/reduce_scatter | solution.py:71
  106.9 41.9 %all-reduce.4.cloned.1.call-done = f32[1,128,128]{2,1,0:T(8,128)} async-done(((f32[1,128,128]{2,1,0:T(8,128)}), f32[1,128,128]{2,1,0:T(8,128)}) %all-reduce.4.cloned.1.call-update) | async-done | bytes 65552 | tf_op jit(solution)/shard_map/psum | solution.py:77
  149.7 868.9 %while.34 = (s32[]{:T(128)}, f32[128,128]{1,0:T(8,128)S(1)}, f32[128,128]{1,0:T(8,128)S(1)}, f32[128,4096]{1,0:T(8,128)}, s32[]{:T(128)}, /*index=5*/s32[32]{0:T...) while((s32[]{:T(128)}, f32[128,128]{1,0:T(8,128)S(1)}, ...), condition=%wide.region_5.6_spmd.clone, body=%wide.region_3.5_spmd.clone.sunk | while | flops 126074896 | bytes 3408247 | solution.py:110
  150.9 107.7 %all-reduce.6.cloned.1.call-done = f32[4,128,128]{2,1,0:T(8,128)} async-done(((f32[4,128,128]{2,1,0:T(8,128)}), f32[4,128,128]{2,1,0:T(8,128)}) %all-reduce.6.cloned.1.call-update) | async-done | bytes 262160 | tf_op jit(solution)/shard_map/while/body/eval_jaxpr/psum | solution.py:98
  262.2 104.5 %all-reduce.6.cloned.1.call-done = f32[4,128,128]{2,1,0:T(8,128)} async-done(((f32[4,128,128]{2,1,0:T(8,128)}), f32[4,128,128]{2,1,0:T(8,128)}) %all-reduce.6.cloned.1.call-update) | async-done | bytes 262160 | tf_op jit(solution)/shard_map/while/body/eval_jaxpr/psum | solution.py:98
  370.3 104.5 %all-reduce.6.cloned.1.call-done = f32[4,128,128]{2,1,0:T(8,128)} async-done(((f32[4,128,128]{2,1,0:T(8,128)}), f32[4,128,128]{2,1,0:T(8,128)}) %all-reduce.6.cloned.1.call-update) | async-done | bytes 262160 | tf_op jit(solution)/shard_map/while/body/eval_jaxpr/psum | solution.py:98
  478.4 104.5 %all-reduce.6.cloned.1.call-done = f32[4,128,128]{2,1,0:T(8,128)} async-done(((f32[4,128,128]{2,1,0:T(8,128)}), f32[4,128,128]{2,1,0:T(8,128)}) %all-reduce.6.cloned.1.call-update) | async-done | bytes 262160 | tf_op jit(solution)/shard_map/while/body/eval_jaxpr/psum | solution.py:98
  586.5 104.8 %all-reduce.6.cloned.1.call-done = f32[4,128,128]{2,1,0:T(8,128)} async-done(((f32[4,128,128]{2,1,0:T(8,128)}), f32[4,128,128]{2,1,0:T(8,128)}) %all-reduce.6.cloned.1.call-update) | async-done | bytes 262160 | tf_op jit(solution)/shard_map/while/body/eval_jaxpr/psum | solution.py:98
  694.9 104.8 %all-reduce.6.cloned.1.call-done = f32[4,128,128]{2,1,0:T(8,128)} async-done(((f32[4,128,128]{2,1,0:T(8,128)}), f32[4,128,128]{2,1,0:T(8,128)}) %all-reduce.6.cloned.1.call-update) | async-done | bytes 262160 | tf_op jit(solution)/shard_map/while/body/eval_jaxpr/psum | solution.py:98
  803.3 104.8 %all-reduce.6.cloned.1.call-done = f32[4,128,128]{2,1,0:T(8,128)} async-done(((f32[4,128,128]{2,1,0:T(8,128)}), f32[4,128,128]{2,1,0:T(8,128)}) %all-reduce.6.cloned.1.call-update) | async-done | bytes 262160 | tf_op jit(solution)/shard_map/while/body/eval_jaxpr/psum | solution.py:98
  911.7 104.5 %all-reduce.6.cloned.1.call-done = f32[4,128,128]{2,1,0:T(8,128)} async-done(((f32[4,128,128]{2,1,0:T(8,128)}), f32[4,128,128]{2,1,0:T(8,128)}) %all-reduce.6.cloned.1.call-update) | async-done | bytes 262160 | tf_op jit(solution)/shard_map/while/body/eval_jaxpr/psum | solution.py:98
  1018.6 852.6 %while.35 = (s32[]{:T(128)}, f32[128,128]{0,1:T(8,128)S(1)}, s32[]{:T(128)}, s32[32]{0:T(128)S(1)}, f32[128,4096]{1,0:T(8,128)}, /*index=5*/s32[]{:T(128)}, f32[...) while((s32[]{:T(128)}, f32[128,128]{0,1:T(8,128)S(1)}, ...), condition=%wide.region_8.9_spmd.clone, body=%wide.region_6.8_spmd.clone.sunk | while | flops 126025744 | bytes 3015076 | solution.py:129
  1018.8 1.5 fusion.90
  1021.2 103.1 %all-reduce.8.cloned.1.call-done = f32[4,128,128]{2,1,0:T(8,128)} async-done(((f32[4,128,128]{2,1,0:T(8,128)}), f32[4,128,128]{2,1,0:T(8,128)}) %all-reduce.8.cloned.1.call-update) | async-done | bytes 262160 | tf_op jit(solution)/shard_map/while/body/eval_jaxpr/psum | solution.py:126
  1128.0 102.8 %all-reduce.8.cloned.1.call-done = f32[4,128,128]{2,1,0:T(8,128)} async-done(((f32[4,128,128]{2,1,0:T(8,128)}), f32[4,128,128]{2,1,0:T(8,128)}) %all-reduce.8.cloned.1.call-update) | async-done | bytes 262160 | tf_op jit(solution)/shard_map/while/body/eval_jaxpr/psum | solution.py:126
  1232.1 1.5 fusion.90
  1234.5 103.1 %all-reduce.8.cloned.1.call-done = f32[4,128,128]{2,1,0:T(8,128)} async-done(((f32[4,128,128]{2,1,0:T(8,128)}), f32[4,128,128]{2,1,0:T(8,128)}) %all-reduce.8.cloned.1.call-update) | async-done | bytes 262160 | tf_op jit(solution)/shard_map/while/body/eval_jaxpr/psum | solution.py:126
  1341.3 102.8 %all-reduce.8.cloned.1.call-done = f32[4,128,128]{2,1,0:T(8,128)} async-done(((f32[4,128,128]{2,1,0:T(8,128)}), f32[4,128,128]{2,1,0:T(8,128)}) %all-reduce.8.cloned.1.call-update) | async-done | bytes 262160 | tf_op jit(solution)/shard_map/while/body/eval_jaxpr/psum | solution.py:126
  1447.8 102.8 %all-reduce.8.cloned.1.call-done = f32[4,128,128]{2,1,0:T(8,128)} async-done(((f32[4,128,128]{2,1,0:T(8,128)}), f32[4,128,128]{2,1,0:T(8,128)}) %all-reduce.8.cloned.1.call-update) | async-done | bytes 262160 | tf_op jit(solution)/shard_map/while/body/eval_jaxpr/psum | solution.py:126
  1551.9 1.5 fusion.90
  1554.3 102.8 %all-reduce.8.cloned.1.call-done = f32[4,128,128]{2,1,0:T(8,128)} async-done(((f32[4,128,128]{2,1,0:T(8,128)}), f32[4,128,128]{2,1,0:T(8,128)}) %all-reduce.8.cloned.1.call-update) | async-done | bytes 262160 | tf_op jit(solution)/shard_map/while/body/eval_jaxpr/psum | solution.py:126
  1658.4 1.5 fusion.90
  1660.8 102.8 %all-reduce.8.cloned.1.call-done = f32[4,128,128]{2,1,0:T(8,128)} async-done(((f32[4,128,128]{2,1,0:T(8,128)}), f32[4,128,128]{2,1,0:T(8,128)}) %all-reduce.8.cloned.1.call-update) | async-done | bytes 262160 | tf_op jit(solution)/shard_map/while/body/eval_jaxpr/psum | solution.py:126
  1767.3 102.8 %all-reduce.8.cloned.1.call-done = f32[4,128,128]{2,1,0:T(8,128)} async-done(((f32[4,128,128]{2,1,0:T(8,128)}), f32[4,128,128]{2,1,0:T(8,128)}) %all-reduce.8.cloned.1.call-update) | async-done | bytes 262160 | tf_op jit(solution)/shard_map/while/body/eval_jaxpr/psum | solution.py:126
  1872.0 1.6 copy.32
  1873.6 46.3 %all-gather.3.cloned.1.call-done = f32[4096,128]{0,1:T(8,128)} async-done(((f32[128,128]{0,1:T(8,128)}), f32[4096,128]{0,1:T(8,128)}) %all-gather.3.cloned.1.call-update) | async-done | bytes 2097168 | tf_op jit(solution)/shard_map/all_gather | solution.py:130
  1919.9 3.9 fusion.34
  1924.3 3.8 fusion.28
  (156 shorter events, 61.4 us)
Async XLA Ops:
  7.2 12.7 copy-start
  7.2 99.7 %reduce-scatter.2.cloned.1.call-start = ((), (), s32[]{:S(2)}) async-start(), calls=%async_computation.1 | async-start | bytes 2162688 | tf_op jit(solution)/shard_map/reduce_scatter | solution.py:71
  12.7 6.6 copy-start.6
  12.7 6.6 copy-start.10
  12.7 6.8 copy-start.8
  26.1 122.7 %copy-start.9 = (f32[1,128,128]{2,1,0:T(8,128)S(1)}, f32[1,128,128]{2,1,0:T(8,128)}, u32[]{:S(2)}) copy-start(f32[1,128,128]{2,1,0:T(8,128)} %param.30) | copy-start | bytes 196612
  26.1 123.6 %copy-start.3 = (f32[1,128,128]{2,1,0:T(8,128)S(1)}, f32[1,128,128]{2,1,0:T(8,128)}, u32[]{:S(2)}) copy-start(f32[1,128,128]{2,1,0:T(8,128)} %param.28) | copy-start | bytes 196612
  26.1 123.6 %copy-start.11 = (s32[1,32]{1,0:T(1,128)S(1)}, s32[1,32]{1,0:T(1,128)}, u32[]{:S(2)}) copy-start(s32[1,32]{1,0:T(1,128)} %param.31) | copy-start | bytes 388
  26.2 122.7 %all-reduce.4.cloned.1.call-start = ((), (), s32[]{:S(2)}) async-start(), calls=%async_computation.2 | async-start | bytes 131072 | tf_op jit(solution)/shard_map/psum | solution.py:77
  149.7 108.9 %all-reduce.6.cloned.1.call-start = ((), (), s32[]{:S(2)}) async-start(), calls=%async_computation.4 | async-start | bytes 524288 | tf_op jit(solution)/shard_map/while/body/eval_jaxpr/psum | solution.py:98
  261.0 105.7 %all-reduce.6.cloned.1.call-start = ((), (), s32[]{:S(2)}) async-start(), calls=%async_computation.4 | async-start | bytes 524288 | tf_op jit(solution)/shard_map/while/body/eval_jaxpr/psum | solution.py:98
  369.1 105.7 %all-reduce.6.cloned.1.call-start = ((), (), s32[]{:S(2)}) async-start(), calls=%async_computation.4 | async-start | bytes 524288 | tf_op jit(solution)/shard_map/while/body/eval_jaxpr/psum | solution.py:98
  477.2 105.7 %all-reduce.6.cloned.1.call-start = ((), (), s32[]{:S(2)}) async-start(), calls=%async_computation.4 | async-start | bytes 524288 | tf_op jit(solution)/shard_map/while/body/eval_jaxpr/psum | solution.py:98
  585.3 106.0 %all-reduce.6.cloned.1.call-start = ((), (), s32[]{:S(2)}) async-start(), calls=%async_computation.4 | async-start | bytes 524288 | tf_op jit(solution)/shard_map/while/body/eval_jaxpr/psum | solution.py:98
  693.7 106.0 %all-reduce.6.cloned.1.call-start = ((), (), s32[]{:S(2)}) async-start(), calls=%async_computation.4 | async-start | bytes 524288 | tf_op jit(solution)/shard_map/while/body/eval_jaxpr/psum | solution.py:98
  802.1 106.0 %all-reduce.6.cloned.1.call-start = ((), (), s32[]{:S(2)}) async-start(), calls=%async_computation.4 | async-start | bytes 524288 | tf_op jit(solution)/shard_map/while/body/eval_jaxpr/psum | solution.py:98
  910.5 105.7 %all-reduce.6.cloned.1.call-start = ((), (), s32[]{:S(2)}) async-start(), calls=%async_computation.4 | async-start | bytes 524288 | tf_op jit(solution)/shard_map/while/body/eval_jaxpr/psum | solution.py:98
  1018.6 105.7 %all-reduce.8.cloned.1.call-start = ((), (), s32[]{:S(2)}) async-start(), calls=%async_computation.5 | async-start | bytes 524288 | tf_op jit(solution)/shard_map/while/body/eval_jaxpr/psum | solution.py:126
  1125.5 105.4 %all-reduce.8.cloned.1.call-start = ((), (), s32[]{:S(2)}) async-start(), calls=%async_computation.5 | async-start | bytes 524288 | tf_op jit(solution)/shard_map/while/body/eval_jaxpr/psum | solution.py:126
  1232.0 105.7 %all-reduce.8.cloned.1.call-start = ((), (), s32[]{:S(2)}) async-start(), calls=%async_computation.5 | async-start | bytes 524288 | tf_op jit(solution)/shard_map/while/body/eval_jaxpr/psum | solution.py:126
  1338.8 105.3 %all-reduce.8.cloned.1.call-start = ((), (), s32[]{:S(2)}) async-start(), calls=%async_computation.5 | async-start | bytes 524288 | tf_op jit(solution)/shard_map/while/body/eval_jaxpr/psum | solution.py:126
  1445.3 105.4 %all-reduce.8.cloned.1.call-start = ((), (), s32[]{:S(2)}) async-start(), calls=%async_computation.5 | async-start | bytes 524288 | tf_op jit(solution)/shard_map/while/body/eval_jaxpr/psum | solution.py:126
  1551.8 105.3 %all-reduce.8.cloned.1.call-start = ((), (), s32[]{:S(2)}) async-start(), calls=%async_computation.5 | async-start | bytes 524288 | tf_op jit(solution)/shard_map/while/body/eval_jaxpr/psum | solution.py:126
  1658.3 105.4 %all-reduce.8.cloned.1.call-start = ((), (), s32[]{:S(2)}) async-start(), calls=%async_computation.5 | async-start | bytes 524288 | tf_op jit(solution)/shard_map/while/body/eval_jaxpr/psum | solution.py:126
  1764.8 105.3 %all-reduce.8.cloned.1.call-start = ((), (), s32[]{:S(2)}) async-start(), calls=%async_computation.5 | async-start | bytes 524288 | tf_op jit(solution)/shard_map/while/body/eval_jaxpr/psum | solution.py:126
  1871.3 0.6 copy-start.2
  1871.3 48.7 %all-gather.3.cloned.1.call-start = ((), (), s32[]{:S(2)}) async-start(), calls=%async_computation.3 | async-start | bytes 2162688 | tf_op jit(solution)/shard_map/all_gather | solution.py:130
  1919.9 4.4 copy-start.1
  1924.3 3.8 copy-start.7
  1924.3 4.2 copy-start.5
  1928.1 1.0 copy-start.4
Sparse Core Ops, SparseCore 0:
  26.3 80.5 reduce-scatter.1
  109.2 39.6 all-reduce.3
  154.7 103.8 all-reduce.5
  265.7 100.9 all-reduce.5
  373.8 100.9 all-reduce.5
  481.9 100.9 all-reduce.5
  590.3 100.9 all-reduce.5
  698.7 100.9 all-reduce.5
  807.1 100.9 all-reduce.5
  915.2 100.9 all-reduce.5
  1023.3 100.9 all-reduce.7
  1129.8 100.9 all-reduce.7
  1236.6 100.9 all-reduce.7
  1343.1 100.9 all-reduce.7
  1449.6 100.9 all-reduce.7
  1556.1 100.9 all-reduce.7
  1662.6 100.9 all-reduce.7
  1769.1 100.9 all-reduce.7
  1875.1 44.7 all-gather.2
where the time goes:
time: 1940 us
  waiting for transfers between devices  1830 us (94%)
  matrix products  58.2 us (3%)
  other arithmetic  23.1 us (1%)
    psum x8, waiting for transfers between devices, forward_step(): solved = lax.psum(pack_slot(candidate, slot, span), 'grid')  840 us
    psum x8, waiting for transfers between devices, back_step(): pulled_group = lax.psum(contribution(group, back_own), 'grid')  823 us
    reduce_scatter x1, waiting for transfers between devices, local(): lax.psum_scatter(summed.reshape(1 * lax.axis_size('grid'), block_width, c...  80.7 us
    all_gather x1, waiting for transfers between devices, local(): shard_piece = lax.all_gather(back_own[None], 'grid', axis=0, tiled=True)  46.3 us
    psum x1, waiting for transfers between devices, local(): reduced = lax.psum(partial_sums, 'layer')  41.9 us
  transfers between devices with their start and end apart: 19, of which 19 were waited for; matrix products, arithmetic and copies ran while one was open for 0% of the time, Pallas kernels for 0%

commit v1 on v0

v1 whole, which is shorter than its diff:
```python
import functools

import jax
import jax.numpy as jnp
from jax import lax
from jax.experimental import pallas as pl
from jax.experimental.pallas import tpu as pltpu
from jax.sharding import PartitionSpec as P

SPAN = 4
KTOP = 32
GROUPS = KTOP // SPAN
BLOCK = 128
KEEP = 14
SLOTS = KEEP + 1


def product(spec, left, right):
    return jnp.einsum(
        spec, left, right, precision=lax.Precision.HIGHEST, preferred_element_type=jnp.float32
    )


def sweep_kernel(rhs_ref, factor_hbm, out_ref, factor, forward, pulled, sems):
    copies = [
        pltpu.make_async_copy(
            factor_hbm.at[pl.ds(d * SLOTS, SLOTS)], factor.at[d], sems.at[d]
        )
        for d in range(KTOP)
    ]
    for copy in copies:
        copy.start()
    eye = lax.broadcasted_iota(jnp.int32, (BLOCK, BLOCK), 0) == lax.broadcasted_iota(
        jnp.int32, (BLOCK, BLOCK), 1
    )

    def fold(value):
        return jnp.broadcast_to(jnp.sum(value, axis=0, keepdims=True), (8, BLOCK))

    def tall(row):
        return jnp.concatenate([row] * (BLOCK // 8), axis=0)

    for i in range(KTOP):
        g = i // SPAN
        copies[i].wait()
        row = jnp.broadcast_to(rhs_ref[pl.ds(i, 1), :], (8, BLOCK))
        acc = jnp.where(eye, tall(row), 0.0)

        def add(j, acc, d, shift):
            return acc + factor[d, j - shift] * tall(forward[j])

        count = min(SPAN * g, KEEP)
        if count:
            acc = lax.fori_loop(
                0, count, functools.partial(add, d=i, shift=0), acc, unroll=2
            )
        if SPAN * g > KEEP:
            acc = lax.fori_loop(
                KEEP,
                SPAN * g,
                functools.partial(add, d=KTOP - 1 - i, shift=SPAN * g - KEEP),
                acc,
                unroll=2,
            )
        column = jnp.sum(acc, axis=1, keepdims=True)
        forward[i] = fold(factor[i, KEEP] * -column)

    pulled[...] = jnp.zeros_like(pulled)
    for i in range(KTOP - 1, -1, -1):
        g = i // SPAN
        row = forward[i] - jnp.broadcast_to(
            jnp.sum(pulled[i], axis=0, keepdims=True), (8, BLOCK)
        )
        column = jnp.sum(factor[i, KEEP] * tall(row), axis=1, keepdims=True)
        wide = jnp.broadcast_to(column, (BLOCK, BLOCK))
        out_ref[pl.ds(i, 1), :] = jnp.sum(jnp.where(eye, wide, 0.0), axis=0, keepdims=True)

        def pull(j, carry, d, shift):
            terms = factor[d, j - shift] * wide
            pulled[j] += jnp.sum(terms.reshape(BLOCK // 8, 8, BLOCK), axis=0)
            return carry

        count = min(SPAN * g, KEEP)
        if count:
            lax.fori_loop(0, count, functools.partial(pull, d=i, shift=0), 0, unroll=2)
        if SPAN * g > KEEP:
            lax.fori_loop(
                KEEP,
                SPAN * g,
                functools.partial(pull, d=KTOP - 1 - i, shift=SPAN * g - KEEP),
                0,
                unroll=2,
            )


def sweep(rhs, factor):
    return pl.pallas_call(
        sweep_kernel,
        out_shape=jax.ShapeDtypeStruct((KTOP, BLOCK), jnp.float32),
        in_specs=[pl.BlockSpec(memory_space=pltpu.VMEM), pl.BlockSpec(memory_space=pl.ANY)],
        out_specs=pl.BlockSpec(memory_space=pltpu.VMEM),
        scratch_shapes=[
            pltpu.VMEM((KTOP, SLOTS, BLOCK, BLOCK), jnp.float32),
            pltpu.VMEM((KTOP, 8, BLOCK), jnp.float32),
            pltpu.VMEM((KTOP, 8, BLOCK), jnp.float32),
            pltpu.SemaphoreType.DMA((KTOP,)),
        ],
        compiler_params=pltpu.CompilerParams(vmem_limit_bytes=44 * 2**20),
    )(rhs, factor)


def pack_rows(factor_row, pattern_row, inverse, position):
    own_group = position // SPAN
    column_groups = jnp.arange(KTOP) // SPAN
    weights = jnp.where(column_groups < own_group, pattern_row, 0).astype(jnp.float32)
    blocks = factor_row.reshape(BLOCK, KTOP, BLOCK).transpose(1, 0, 2) * weights[:, None, None]
    start = jnp.maximum(SPAN * own_group - KEEP, 0)
    excess = lax.dynamic_slice_in_dim(blocks, start, KEEP)
    got = lax.ppermute(excess, "grid", [(KTOP - 1 - d, d) for d in range(KTOP // 2)])
    own = (jnp.arange(KEEP) < SPAN * own_group)[:, None, None]
    packed = jnp.where(own, blocks[:KEEP], got)
    return jnp.concatenate([packed, inverse.T[None]], axis=0)


def local(
    leaf_inverse,
    leaf_coupling,
    leaf_rhs,
    mid_inverse,
    mid_coupling,
    mid_rhs,
    mid_top,
    root_inverse,
    root_top,
    root_rhs,
    top_inverse,
    top_factor,
    top_rhs,
    top_pattern,
):
    columns = leaf_rhs.shape[-1]
    position = lax.axis_index("grid")
    layer = lax.axis_index("layer")
    layers = lax.axis_size("layer")
    packed = pack_rows(top_factor[0], top_pattern[0], top_inverse[0], position)
    factor = lax.all_gather(packed, "grid", axis=0, tiled=True)

    leaf_inv = leaf_inverse[0, 0]
    leaf_links = leaf_coupling[0, 0]
    forward_leaf = product("pab,pbr->par", leaf_inv, leaf_rhs[0, 0])
    pulled = (
        product("pab,pbr->par", leaf_links, forward_leaf)
        .reshape(-1, 2, BLOCK, columns)
        .sum(axis=1)
    )
    forward_mid = product("mab,mbr->mar", mid_inverse[0, 0], mid_rhs[0, 0] - pulled)
    root_input = root_rhs[0, 0] - product("mab,mbr->ar", mid_coupling[0, 0], forward_mid)
    forward_root = product("ab,br->ar", root_inverse[0, 0], root_input)
    root_panel = root_top[0, 0]
    mid_panel = mid_top[0, 0]
    summed = product("br,kb->rk", forward_root, root_panel) + product(
        "mbr,mkb->rk", forward_mid, mid_panel
    )
    summed = summed.reshape(columns, KTOP, BLOCK)
    mine = ((jnp.arange(KTOP) == position) & (layer == 0))[None, :, None]
    summed = summed - jnp.where(mine, top_rhs[0].T[:, None, :], 0.0)
    summed = summed.reshape(KTOP, layers, KTOP, BLOCK).transpose(1, 0, 2, 3)
    summed = summed.reshape(columns, KTOP, BLOCK)
    parts = lax.all_to_all(summed, ("layer", "grid"), 0, 0, tiled=True)
    residual = parts.sum(axis=0)

    own_column = sweep(residual, factor)
    layer_columns = lax.all_gather(own_column, "layer", axis=0)
    grid = lax.axis_size("grid")
    everywhere = jnp.broadcast_to(layer_columns[None], (grid, layers, KTOP, BLOCK))
    solved = lax.all_to_all(everywhere, "grid", 0, 0, tiled=True)
    solved = solved.reshape(columns, KTOP, BLOCK)
    own_top = lax.dynamic_index_in_dim(solved, position, 1, keepdims=False).T
    flat = solved.reshape(columns, KTOP * BLOCK)
    root_pull = product("kb,rk->br", root_panel, flat)
    mid_pull = product("mkb,rk->mbr", mid_panel, flat)
    back_root = product("ba,br->ar", root_inverse[0, 0], forward_root - root_pull)
    back_mid = product(
        "mba,mbr->mar",
        mid_inverse[0, 0],
        forward_mid - product("mab,ar->mbr", mid_coupling[0, 0], back_root) - mid_pull,
    )
    parent = jnp.repeat(back_mid, 2, axis=0)
    back_leaf = product(
        "pba,pbr->par", leaf_inv, forward_leaf - product("pab,par->pbr", leaf_links, parent)
    )
    return (back_leaf[None, None], back_mid[None, None], back_root[None, None], own_top[None])


def solution(mesh):
    placed = (
        P("layer", "grid", None, None, None),
        P("layer", "grid", None, None, None),
        P("layer", "grid", None, None, None),
        P("layer", "grid", None, None, None),
        P("layer", "grid", None, None, None),
        P("layer", "grid", None, None, None),
        P("layer", "grid", None, None, None),
        P("layer", "grid", None, None),
        P("layer", "grid", None, None),
        P("layer", "grid", None, None),
        P("grid", None, None),
        P("grid", None, None),
        P("grid", None, None),
        P("grid", None),
    )
    return jax.shard_map(
        local,
        mesh=mesh,
        in_specs=placed,
        out_specs=(
            P("layer", "grid", None, None, None),
            P("layer", "grid", None, None, None),
            P("layer", "grid", None, None),
            P("grid", None, None),
        ),
        check_vma=False,
    )
```

time: 1940 us -> 265 us (0.14)
  waiting for transfers between devices: 1830 us -> 126 us
  blocking collectives: 0 us -> 47.9 us
  matrix products: 58.2 us -> 26.1 us
    psum x17 -> x0, waiting for transfers between devices: 1710 us -> none  [the longest x8 840 us: forward_step(): solved = lax.psum(pack_slot(candidate, slot, span), 'grid')]
    reduce_scatter x1 -> x0, waiting for transfers between devices: 80.7 us -> none  [local(): lax.psum_scatter(summed.reshape(1 * lax.axis_size('grid'), block_width, c...]
    all_to_all x0 -> x1, blocking collectives: none -> 38.3 us  [local(): parts = lax.all_to_all(summed, ('layer', 'grid'), 0, 0, tiled=True)]
    dot_general x33 -> x0, matrix products: 37.7 us -> none  [the longest x17 25.2 us: transposed(): lax.dot_general(left, right, (((0,), (0,)), ((), ())), precision=lax.Prec...]
    all_to_all x0 -> x1, waiting for transfers between devices: none -> 28.3 us  [local(): solved = lax.all_to_all(everywhere, 'grid', 0, 0, tiled=True)]
    ppermute x0 -> x1, waiting for transfers between devices: none -> 27.1 us  [pack_rows(): lax.ppermute(excess, 'grid', [(KTOP - 1 - d, d) for d in range(KTOP // 2)])]
    all_gather x1, waiting for transfers between devices: 46.3 us -> 70.9 us  [local(): factor = lax.all_gather(packed, 'grid', axis=0, tiled=True)]
  transfers between devices with their start and end apart: 19 -> 3, of which waited for: 19 -> 3; matrix products, arithmetic and copies ran while one was open for 0% -> 8% of each run, Pallas kernels for 0% -> 0%
where the time goes in v1:
time: 265 us; the launch traced here: 264 us
  waiting for transfers between devices  126 us (48%)
  blocking collectives  47.9 us (18%)
  matrix products  26.1 us (10%)
  Pallas kernels  18.2 us (7%)
  local copies, waits for them, and re-layouts  16.5 us (6%)
  between operations  14.4 us (5%)
  starting transfers between devices  9.17 us (3%)
  other arithmetic  5.42 us (2%)
    all_gather x1, waiting for transfers between devices, local(): factor = lax.all_gather(packed, 'grid', axis=0, tiled=True)  70.9 us
    all_to_all x1, blocking collectives, local(): parts = lax.all_to_all(summed, ('layer', 'grid'), 0, 0, tiled=True)  38.3 us
    all_to_all x1, waiting for transfers between devices, local(): solved = lax.all_to_all(everywhere, 'grid', 0, 0, tiled=True)  28.3 us
    ppermute x1, waiting for transfers between devices, pack_rows(): lax.ppermute(excess, 'grid', [(KTOP - 1 - d, d) for d in range(KTOP // 2)])  27.1 us
    dot_general x14, matrix products, product(): jnp.einsum(spec, left, right, precision=lax.Precision.HIGHEST, preferred_...  26.1 us
    pallas_call x1, Pallas kernels, sweep(): pl.pallas_call(sweep_kernel, out_shape=jax.ShapeDtypeStruct((KTOP, BLOCK)...  18.2 us
    unnamed x29, local copies, waits for them, and re-layouts  9.71 us
    all_gather x1, blocking collectives, local(): layer_columns = lax.all_gather(own_column, 'layer', axis=0)  9.63 us
  transfers between devices with their start and end apart: 3, of which 3 were waited for; matrix products, arithmetic and copies ran while one was open for 8% of the time, Pallas kernels for 0%

profile of v1, /device:TPU:1, one launch (start us, length us, event | category | flops | bytes accessed | tf_op | source)
XLA Modules:
  0.0 264.1 jit_solution(12146060372277664946)
XLA Ops:
  7.2 0.8 fusion.44
  8.0 2.9 %copy.62 = f32[1,128,4096]{1,2,0:T(8,128)} copy(f32[1,128,4096]{2,1,0:T(8,128)} %param.25) | data formatting | bytes 4194304 | tf_op args[11]
  11.0 1.9 broadcast_multiply_fusion
  13.0 1.3 collective-permute-start
  14.5 27.1 %collective-permute-done = f32[14,128,128]{1,2,0:T(8,128)S(1)} collective-permute-done((f32[14,128,128]{1,2,0:T(8,128)S(1)}, f32[14,128,128]{1,2,0:T(8,128)S(1)}, u32[]{:S(2)}, u32[]{:S(2)}) %collective-permute-start) | collective-permute-done | bytes 917536 | tf_op jit(solution)/shard_map/ppermute | solution.py:119
  42.0 1.3 copy.63
  43.3 0.7 copy.58
  44.0 0.9 copy.59
  45.0 1.7 copy.56
  46.6 1.3 fusion.30
  48.6 1.3 convolution_bitcast_fusion.4
  49.9 1.1 fusion.24
  51.0 1.1 fusion.42
  52.2 7.0 %convolution_bitcast_fusion = f32[128,4096]{1,0:T(8,128)S(1)} fusion(f32[2,128,128]{1,2,0:T(8,128)S(1)} %convolution_bitcast_fusion.4, f32[1,1,2,4096,128]{4,3,2,1,0:T(8,128)} %param.20), kind=kOutput, calls=%fused_computation | convolution fusion | flops 1610612736 | bytes 6422528 | tf_op jit(solution)/shard_map/mbr,mkb->rk/dot_general | solution.py:19
  59.1 2.0 fusion.8
  62.0 38.3 %all_to_all.10 = f32[128,32,128]{2,1,0:T(8,128)} all-to-all(f32[128,32,128]{2,1,0:T(8,128)S(1)} %bitcast.146), channel_id=1, replica_groups=mesh['layer'=4,'grid'=32] {'layer','grid'}, dimensions={0} | all-to-all | bytes 4194304 | tf_op jit(solution)/shard_map/all_to_all | solution.py:169
  100.3 1.8 reduce_sum.19.rhs_ref
  102.0 70.9 %all-gather.3.cloned.1.call-done.factor_hbm = f32[480,128,128]{2,1,0:T(8,128)} async-done(((f32[15,128,128]{2,1,0:T(8,128)}), f32[480,128,128]{2,1,0:T(8,128)}) %all-gather.3.cloned.1.call-update) | async-done | bytes 31457296 | tf_op jit(solution)/shard_map/all_gather | solution.py:146
  172.9 18.2 %shard_map.165 = f32[32,128]{1,0:T(8,128)S(1)} custom-call(f32[32,128]{1,0:T(8,128)S(1)} %reduce_sum.19.rhs_ref, f32[480,128,128]{2,1,0:T(8,128)} %all-gather.3.cloned.1.call-done.factor_hbm), custom_call_target="tpu_custom_call" | custom-call | tf_op jit(solution)/shard_map/pallas_call | solution.py:97
  191.2 9.6 %all-gather = f32[128,128]{1,0:T(8,128)S(1)} all-gather(f32[32,128]{1,0:T(8,128)S(1)} %shard_map.165), channel_id=2, replica_groups=mesh['layer'=4,'grid'=32] {'layer'}, dimensions={0}, use_global_device_ids=true | all-gather | bytes 81920 | tf_op jit(solution)/shard_map/all_gather | solution.py:173
  200.8 1.6 broadcast_in_dim.66
  202.4 7.8 %all-to-all-start.1 = ((f32[32,4,32,128]{3,2,1,0:T(8,128)}), f32[32,4,32,128]{3,2,1,0:T(8,128)}, u32[]{:S(2)}, u32[]{:S(2)}) async-start(f32[32,4,32,128]{3,2,1,0:T(8,128)} %broadcast_in_dim.66), calls=%async_computation.1 | async-start | bytes 4194304 | tf_op jit(solution)/shard_map/all_to_all | solution.py:176
  210.2 28.3 %all-to-all-done.1 = f32[32,4,32,128]{3,2,1,0:T(8,128)} async-done(((f32[32,4,32,128]{3,2,1,0:T(8,128)}), f32[32,4,32,128]{3,2,1,0:T(8,128)}, u32[]{:S(2)}, u32[]{:S(2)}) %all-to-all-start.1) | async-done | bytes 2097184 | tf_op jit(solution)/shard_map/all_to_all | solution.py:176
  238.6 4.8 %fusion.19 = f32[128,128]{1,0:T(8,128)S(1)} fusion(f32[128,128]{1,0:T(8,128)S(1)} %fusion.42, f32[1,1,4096,128]{3,2,1,0:T(8,128)S(1)} %copy-done, f32[16,8,32,128]{3,2,1,0:T(8,128)} %bitcast.60), kind=kOutput, calls=%fused_computation.20 | convolution fusion | flops 805322752 | bytes 4325376 | tf_op jit(solution)/shard_map/kb,rk->br/dot_general | solution.py:19
  243.9 1.1 constant_dynamic-slice_fusion
  245.0 0.7 copy.69
  245.7 0.7 copy.68
  246.4 2.7 %reshape.67 = f32[128,4096,1]{1,0,2:T(8,128)} reshape(f32[32,4,32,128]{3,2,1,0:T(8,128)} %all-to-all-done.1) | data formatting | bytes 4194304 | tf_op jit(solution)/shard_map/reshape;reshape | solution.py:179
  249.2 4.9 %fusion.15 = f32[2,128,128]{1,2,0:T(8,128)S(1)} fusion(f32[2,128,128]{1,2,0:T(8,128)S(1)} %fusion.18, f32[128,4096,1]{1,0,2:T(8,128)} %reshape.67, f32[1,1,2,4096,128]{4,3,2,1,0:T(8,128)} %param.20), kind=kOutput, calls=%fused_computation.16 | convolution fusion | flops 1610645504 | bytes 6553600 | tf_op jit(solution)/shard_map/mkb,rk->mbr/dot_general | solution.py:19
  254.4 0.8 copy.67
  255.2 0.6 fusion.11
  256.4 0.8 copy.66
  (37 shorter events, 3.4 us)
Async XLA Ops:
  7.2 52.0 %copy-start = (f32[1,1,4096,128]{3,2,1,0:T(8,128)S(1)}, f32[1,1,4096,128]{3,2,1,0:T(8,128)}, u32[]{:S(2)}) copy-start(f32[1,1,4096,128]{3,2,1,0:T(8,128)} %param.22) | copy-start | bytes 6291460
  7.2 165.7 %all-gather.3.cloned.1.call-start = ((), (), s32[]{:S(2)}) async-start(), calls=%async_computation.2 | async-start | bytes 32440320 | tf_op jit(solution)/shard_map/all_gather | solution.py:146
  11.0 3.3 %copy-start.1 = (f32[1,128,4096]{1,2,0:T(8,128)S(1)}, f32[1,128,4096]{1,2,0:T(8,128)}, u32[]{:S(2)}) copy-start(f32[1,128,4096]{1,2,0:T(8,128)} %copy.62) | copy-start | bytes 6291460
  13.0 28.7 %collective-permute-start = (f32[14,128,128]{1,2,0:T(8,128)S(1)}, f32[14,128,128]{1,2,0:T(8,128)S(1)}, u32[]{:S(2)}, u32[]{:S(2)}) collective-permute-start(f32[14,128,128]{1,2,0:T(8,128)S(1)} %dynamic-slice_bitcast_fusion), channel_id=1, source_target_pairs={{31,0},{30,1},{29,2},{28,3},{27,4},{26,5},{25,6},{24,7},{23,8},{22... | collective-permute-start | bytes 2752520 | tf_op jit(solution)/shard_map/ppermute | solution.py:119
  14.5 27.3 %copy-start.8 = (f32[1,128,128]{2,1,0:T(8,128)S(1)}, f32[1,128,128]{2,1,0:T(8,128)}, u32[]{:S(2)}) copy-start(f32[1,128,128]{2,1,0:T(8,128)} %param.24) | copy-start | bytes 196612
  41.8 1.5 copy-start.9
  41.9 4.7 %copy-start.2 = (f32[1,1,4,128,128]{4,3,2,1,0:T(8,128)S(1)}, f32[1,1,4,128,128]{4,3,2,1,0:T(8,128)}, u32[]{:S(2)}) copy-start(f32[1,1,4,128,128]{4,3,2,1,0:T(8,128)} %param.14) | copy-start | bytes 786436
  42.0 6.7 %copy-start.5 = (f32[1,1,2,128,128]{4,3,2,1,0:T(8,128)S(1)}, f32[1,1,2,128,128]{4,3,2,1,0:T(8,128)}, u32[]{:S(2)}) copy-start(f32[1,1,2,128,128]{4,3,2,1,0:T(8,128)} %param.17) | copy-start | bytes 393220
  43.3 4.7 %copy-start.3 = (f32[1,1,4,128,128]{4,3,2,1,0:T(8,128)S(1)}, f32[1,1,4,128,128]{4,3,2,1,0:T(8,128)}, u32[]{:S(2)}) copy-start(f32[1,1,4,128,128]{4,3,2,1,0:T(8,128)} %param.15) | copy-start | bytes 786436
  43.3 6.7 %copy-start.4 = (f32[1,1,2,128,128]{4,3,2,1,0:T(8,128)S(1)}, f32[1,1,2,128,128]{4,3,2,1,0:T(8,128)}, u32[]{:S(2)}) copy-start(f32[1,1,2,128,128]{4,3,2,1,0:T(8,128)} %param.18) | copy-start | bytes 393220
  202.4 36.2 %all-to-all-start.1 = ((f32[32,4,32,128]{3,2,1,0:T(8,128)}), f32[32,4,32,128]{3,2,1,0:T(8,128)}, u32[]{:S(2)}, u32[]{:S(2)}) async-start(f32[32,4,32,128]{3,2,1,0:T(8,128)} %broadcast_in_dim.66), calls=%async_computation.1 | async-start | bytes 4194304 | tf_op jit(solution)/shard_map/all_to_all | solution.py:176
  238.6 4.8 %copy-start.7 = (f32[1,1,128,128]{3,2,1,0:T(8,128)S(1)}, f32[1,1,128,128]{3,2,1,0:T(8,128)}, u32[]{:S(2)}) copy-start(f32[1,1,128,128]{3,2,1,0:T(8,128)} %param.21) | copy-start | bytes 196612
  249.2 5.0 %copy-start.6 = (f32[1,1,2,128,128]{4,3,2,1,0:T(8,128)S(1)}, f32[1,1,2,128,128]{4,3,2,1,0:T(8,128)}, u32[]{:S(2)}) copy-start(f32[1,1,2,128,128]{4,3,2,1,0:T(8,128)} %param.17) | copy-start | bytes 393220
Sparse Core Ops, SparseCore 0:
  43.4 129.4 all-gather.2

commit v2 on v1

--- a/solution.py
+++ b/solution.py
@@ -5,8 +5,9 @@
 from jax import lax
 from jax.experimental import pallas as pl
 from jax.experimental.pallas import tpu as pltpu
-from jax.sharding import PartitionSpec as P
-
+from jax.sharding import Mesh, PartitionSpec as P
+
+GRID = ("chip", "core")
 SPAN = 4
 KTOP = 32
 GROUPS = KTOP // SPAN
@@ -22,14 +23,20 @@
 
 
 def sweep_kernel(rhs_ref, factor_hbm, out_ref, factor, forward, pulled, sems):
+    layers = factor_hbm.shape[0] // KTOP
+    part = BLOCK // layers
     copies = [
-        pltpu.make_async_copy(
-            factor_hbm.at[pl.ds(d * SLOTS, SLOTS)], factor.at[d], sems.at[d]
-        )
+        [
+            pltpu.make_async_copy(
+                factor_hbm.at[l * KTOP + d], factor.at[d, :, pl.ds(l * part, part)], sems.at[d, l]
+            )
+            for l in range(layers)
+        ]
         for d in range(KTOP)
     ]
-    for copy in copies:
-        copy.start()
+    for row_copies in copies:
+        for copy in row_copies:
+            copy.start()
     eye = lax.broadcasted_iota(jnp.int32, (BLOCK, BLOCK), 0) == lax.broadcasted_iota(
         jnp.int32, (BLOCK, BLOCK), 1
     )
@@ -42,7 +49,8 @@
 
     for i in range(KTOP):
         g = i // SPAN
-        copies[i].wait()
+        for copy in copies[i]:
+            copy.wait()
         row = jnp.broadcast_to(rhs_ref[pl.ds(i, 1), :], (8, BLOCK))
         acc = jnp.where(eye, tall(row), 0.0)
 
@@ -103,23 +111,30 @@
             pltpu.VMEM((KTOP, SLOTS, BLOCK, BLOCK), jnp.float32),
             pltpu.VMEM((KTOP, 8, BLOCK), jnp.float32),
             pltpu.VMEM((KTOP, 8, BLOCK), jnp.float32),
-            pltpu.SemaphoreType.DMA((KTOP,)),
+            pltpu.SemaphoreType.DMA((KTOP, factor.shape[0] // KTOP)),
         ],
         compiler_params=pltpu.CompilerParams(vmem_limit_bytes=44 * 2**20),
     )(rhs, factor)
 
 
-def pack_rows(factor_row, pattern_row, inverse, position):
+def pack_rows(factor_row, pattern_row, inverse, position, layer, layers):
+    part = BLOCK // layers
     own_group = position // SPAN
     column_groups = jnp.arange(KTOP) // SPAN
     weights = jnp.where(column_groups < own_group, pattern_row, 0).astype(jnp.float32)
-    blocks = factor_row.reshape(BLOCK, KTOP, BLOCK).transpose(1, 0, 2) * weights[:, None, None]
+    rows = lax.dynamic_slice_in_dim(factor_row, layer * part, part)
+    blocks = rows.reshape(part, KTOP, BLOCK).transpose(1, 0, 2) * weights[:, None, None]
     start = jnp.maximum(SPAN * own_group - KEEP, 0)
     excess = lax.dynamic_slice_in_dim(blocks, start, KEEP)
-    got = lax.ppermute(excess, "grid", [(KTOP - 1 - d, d) for d in range(KTOP // 2)])
+    got = lax.ppermute(excess, GRID, [(KTOP - 1 - d, d) for d in range(KTOP // 2)])
     own = (jnp.arange(KEEP) < SPAN * own_group)[:, None, None]
     packed = jnp.where(own, blocks[:KEEP], got)
-    return jnp.concatenate([packed, inverse.T[None]], axis=0)
+    diagonal = lax.dynamic_slice_in_dim(inverse.T, layer * part, part)
+    return jnp.concatenate([packed, diagonal[None]], axis=0)
+
+
+def swap_cores(value):
+    return lax.ppermute(value, "core", [(0, 1), (1, 0)])
 
 
 def local(
@@ -139,11 +154,15 @@
     top_pattern,
 ):
     columns = leaf_rhs.shape[-1]
-    position = lax.axis_index("grid")
+    half = columns // 2
+    position = lax.axis_index(GRID)
+    core = lax.axis_index("core")
     layer = lax.axis_index("layer")
     layers = lax.axis_size("layer")
-    packed = pack_rows(top_factor[0], top_pattern[0], top_inverse[0], position)
-    factor = lax.all_gather(packed, "grid", axis=0, tiled=True)
+    packed = pack_rows(
+        top_factor[0], top_pattern[0], top_inverse[0], position, layer, layers
+    )
+    factor = lax.all_gather(packed, ("layer",) + GRID, axis=0)
 
     leaf_inv = leaf_inverse[0, 0]
     leaf_links = leaf_coupling[0, 0]
@@ -164,17 +183,18 @@
     summed = summed.reshape(columns, KTOP, BLOCK)
     mine = ((jnp.arange(KTOP) == position) & (layer == 0))[None, :, None]
     summed = summed - jnp.where(mine, top_rhs[0].T[:, None, :], 0.0)
-    summed = summed.reshape(KTOP, layers, KTOP, BLOCK).transpose(1, 0, 2, 3)
-    summed = summed.reshape(columns, KTOP, BLOCK)
-    parts = lax.all_to_all(summed, ("layer", "grid"), 0, 0, tiled=True)
+    away = lax.dynamic_slice_in_dim(summed, (1 - core) * half, half)
+    home = lax.dynamic_slice_in_dim(summed, core * half, half)
+    parts = lax.all_to_all(home + swap_cores(away), ("layer", "chip"), 0, 0, tiled=True)
     residual = parts.sum(axis=0)
 
     own_column = sweep(residual, factor)
-    layer_columns = lax.all_gather(own_column, "layer", axis=0)
-    grid = lax.axis_size("grid")
-    everywhere = jnp.broadcast_to(layer_columns[None], (grid, layers, KTOP, BLOCK))
-    solved = lax.all_to_all(everywhere, "grid", 0, 0, tiled=True)
-    solved = solved.reshape(columns, KTOP, BLOCK)
+    everywhere = jnp.broadcast_to(own_column[None], (half, KTOP, BLOCK))
+    near = lax.all_to_all(everywhere, ("layer", "chip"), 0, 0, tiled=True)
+    far = swap_cores(near)
+    solved = jnp.concatenate(
+        [jnp.where(core == 0, near, far), jnp.where(core == 0, far, near)], axis=0
+    )
     own_top = lax.dynamic_index_in_dim(solved, position, 1, keepdims=False).T
     flat = solved.reshape(columns, KTOP * BLOCK)
     root_pull = product("kb,rk->br", root_panel, flat)
@@ -193,31 +213,34 @@
 
 
 def solution(mesh):
+    layers, grid = mesh.devices.shape
+    chips = Mesh(mesh.devices.reshape(layers, grid // 2, 2), ("layer",) + GRID)
+    subtree = ("layer", GRID)
     placed = (
-        P("layer", "grid", None, None, None),
-        P("layer", "grid", None, None, None),
-        P("layer", "grid", None, None, None),
-        P("layer", "grid", None, None, None),
-        P("layer", "grid", None, None, None),
-        P("layer", "grid", None, None, None),
-        P("layer", "grid", None, None, None),
-        P("layer", "grid", None, None),
-        P("layer", "grid", None, None),
-        P("layer", "grid", None, None),
-        P("grid", None, None),
-        P("grid", None, None),
-        P("grid", None, None),
-        P("grid", None),
+        P(*subtree, None, None, None),
+        P(*subtree, None, None, None),
+        P(*subtree, None, None, None),
+        P(*subtree, None, None, None),
+        P(*subtree, None, None, None),
+        P(*subtree, None, None, None),
+        P(*subtree, None, None, None),
+        P(*subtree, None, None),
+        P(*subtree, None, None),
+        P(*subtree, None, None),
+        P(GRID, None, None),
+        P(GRID, None, None),
+        P(GRID, None, None),
+        P(GRID, None),
     )
     return jax.shard_map(
         local,
-        mesh=mesh,
+        mesh=chips,
         in_specs=placed,
         out_specs=(
-            P("layer", "grid", None, None, None),
-            P("layer", "grid", None, None, None),
-            P("layer", "grid", None, None),
-            P("grid", None, None),
+            P(*subtree, None, None, None),
+            P(*subtree, None, None, None),
+            P(*subtree, None, None),
+            P(GRID, None, None),
         ),
         check_vma=False,
     )

time: 265 us -> 220 us (0.83)
  waiting for transfers between devices: 126 us -> 73.5 us
  blocking collectives: 47.9 us -> 59.7 us
  starting transfers between devices: 9.17 us -> 3.57 us
  other arithmetic: 5.42 us -> 9.02 us
  matrix products: 26.1 us -> 22.8 us
    all_to_all x1 -> x0, waiting for transfers between devices: 28.3 us -> none  [local(): solved = lax.all_to_all(everywhere, 'grid', 0, 0, tiled=True)]
    all_to_all x1 -> x2, blocking collectives: 38.3 us -> 59.7 us  [the longest x1 34.1 us: local(): lax.all_to_all(home + swap_cores(away), ('layer', 'chip'), 0, 0, tiled=True)]
    all_gather x1, waiting for transfers between devices: 70.9 us -> 55.1 us  [local(): factor = lax.all_gather(packed, ('layer',) + GRID, axis=0)]
    all_gather x1 -> x0, blocking collectives: 9.63 us -> none  [local(): layer_columns = lax.all_gather(own_column, 'layer', axis=0)]
    ppermute x1 -> x3, waiting for transfers between devices: 27.1 us -> 18.4 us  [the longest x1 13.2 us: pack_rows(): lax.ppermute(excess, GRID, [(KTOP - 1 - d, d) for d in range(KTOP // 2)])]
    all_to_all x1 -> x0, starting transfers between devices: 7.84 us -> none  [local(): solved = lax.all_to_all(everywhere, 'grid', 0, 0, tiled=True)]
    dot_general x14, matrix products: 26.1 us -> 22.8 us  [product(): jnp.einsum(spec, left, right, precision=lax.Precision.HIGHEST, preferred_...]
    reshape x0 -> x1, local copies, waits for them, and re-layouts: none -> 2.75 us  [local(): flat = solved.reshape(columns, KTOP * BLOCK)]
  transfers between devices with their start and end apart: 3 -> 4, of which waited for: 3 -> 4; matrix products, arithmetic and copies ran while one was open for 8% -> 9% of each run, Pallas kernels for 0% -> 0%
where the time goes in v2:
time: 220 us; the launch traced here: 219 us
  waiting for transfers between devices  73.5 us (33%)
  blocking collectives  59.7 us (27%)
  matrix products  22.8 us (10%)
  Pallas kernels  19.2 us (9%)
  local copies, waits for them, and re-layouts  16.9 us (8%)
  between operations  14.5 us (7%)
  other arithmetic  9.02 us (4%)
  starting transfers between devices  3.57 us (2%)
    all_gather x1, waiting for transfers between devices, local(): factor = lax.all_gather(packed, ('layer',) + GRID, axis=0)  55.1 us
    all_to_all x1, blocking collectives, local(): lax.all_to_all(home + swap_cores(away), ('layer', 'chip'), 0, 0, tiled=True)  34.1 us
    all_to_all x1, blocking collectives, local(): near = lax.all_to_all(everywhere, ('layer', 'chip'), 0, 0, tiled=True)  25.6 us
    dot_general x14, matrix products, product(): jnp.einsum(spec, left, right, precision=lax.Precision.HIGHEST, preferred_...  22.8 us
    pallas_call x1, Pallas kernels, sweep(): pl.pallas_call(sweep_kernel, out_shape=jax.ShapeDtypeStruct((KTOP, BLOCK)...  19.2 us
    ppermute x1, waiting for transfers between devices, pack_rows(): lax.ppermute(excess, GRID, [(KTOP - 1 - d, d) for d in range(KTOP // 2)])  13.2 us
    unnamed x52, local copies, waits for them, and re-layouts  10.5 us
    ppermute x2, waiting for transfers between devices, swap_cores(): return lax.ppermute(value, 'core', [(0, 1), (1, 0)])  5.19 us
  transfers between devices with their start and end apart: 4, of which 4 were waited for; matrix products, arithmetic and copies ran while one was open for 9% of the time, Pallas kernels for 0%

profile of v2, /device:TPU:1, one launch (start us, length us, event | category | flops | bytes accessed | tf_op | source)
XLA Modules:
  0.0 219.3 jit_solution(13106317346734902881)
XLA Ops:
  7.3 1.2 dynamic-slice_bitcast_fusion
  8.8 1.4 collective-permute-start.1
  10.5 13.2 %collective-permute-done.1 = f32[14,32,128]{2,0,1:T(8,128)} collective-permute-done((f32[14,32,128]{2,0,1:T(8,128)S(1)}, f32[14,32,128]{2,0,1:T(8,128)}, u32[]{:S(2)}, u32[]{:S(2)}) %collective-permute-start.1) | collective-permute-done | bytes 229408 | tf_op jit(solution)/shard_map/ppermute | solution.py:129
  23.7 1.0 slice_select_fusion
  24.8 0.8 copy.52
  25.7 1.6 copy.49
  27.3 1.3 fusion.30
  29.3 1.3 convolution_bitcast_fusion.4
  30.6 1.1 fusion.24
  32.0 6.5 %convolution_bitcast_fusion = f32[128,4096]{1,0:T(8,128)S(1)} fusion(f32[2,128,128]{1,2,0:T(8,128)S(1)} %convolution_bitcast_fusion.4, f32[1,1,2,4096,128]{4,3,2,1,0:T(8,128)} %param.20), kind=kOutput, calls=%fused_computation | convolution fusion | flops 1610612736 | bytes 6422528 | tf_op jit(solution)/shard_map/mbr,mkb->rk/dot_general | solution.py:20
  38.5 2.0 fusion.8
  40.5 1.7 copy.69
  42.3 2.0 bitcast_subtract_fusion
  44.3 1.3 copy-done.2
  45.8 2.8 %collective-permute-done = f32[64,32,128]{2,1,0:T(8,128)} collective-permute-done((f32[64,32,128]{2,1,0:T(8,128)S(1)}, f32[64,32,128]{2,1,0:T(8,128)}, u32[]{:S(2)}, u32[]{:S(2)}) %collective-permute-start) | collective-permute-done | bytes 1048608 | tf_op jit(solution)/shard_map/ppermute | solution.py:137
  48.5 1.7 dynamic-slice_add_fusion
  50.3 34.1 %all_to_all.10 = f32[64,32,128]{2,1,0:T(8,128)S(1)} all-to-all(f32[64,32,128]{2,1,0:T(8,128)S(1)} %dynamic-slice_add_fusion), channel_id=1, replica_groups=mesh['layer'=4,'chip'=16,'core'=2] {'layer','chip'}, dimensions={0} | all-to-all | bytes 2097152 | tf_op jit(solution)/shard_map/all_to_all | solution.py:188
  84.5 55.1 %all-gather.3.cloned.1.call-done = f32[1920,32,128]{2,1,0:T(8,128)} async-done(((f32[15,32,128]{2,1,0:T(8,128)}), f32[1920,32,128]{2,1,0:T(8,128)}) %all-gather.3.cloned.1.call-update) | async-done | bytes 31457296 | tf_op jit(solution)/shard_map/all_gather | solution.py:165
  139.6 19.2 %shard_map.165 = f32[32,128]{1,0:T(8,128)S(1)} custom-call(f32[32,128]{1,0:T(8,128)S(1)} %reduce_sum.19.rhs_ref, f32[128,15,32,128]{3,2,1,0:T(8,128)} %bitcast.139), custom_call_target="tpu_custom_call" | custom-call | tf_op jit(solution)/shard_map/pallas_call | solution.py:105
  158.9 25.6 %all_to_all.11 = f32[64,32,128]{2,1,0:T(8,128)S(1)} all-to-all(f32[64,32,128]{2,1,0:T(8,128)S(1)} %broadcast_in_dim.63), channel_id=1, replica_groups=mesh['layer'=4,'chip'=16,'core'=2] {'layer','chip'}, dimensions={0} | all-to-all | bytes 2097152 | tf_op jit(solution)/shard_map/all_to_all | solution.py:193
  184.5 2.0 collective-permute-start.2
  186.5 2.4 %collective-permute-done.2 = f32[64,32,128]{2,1,0:T(8,128)} collective-permute-done((f32[64,32,128]{2,1,0:T(8,128)S(1)}, f32[64,32,128]{2,1,0:T(8,128)}, u32[]{:S(2)}, u32[]{:S(2)}) %collective-permute-start.2) | collective-permute-done | bytes 1048608 | tf_op jit(solution)/shard_map/ppermute | solution.py:137
  188.9 2.7 %copy_select_fusion.1 = (f32[64,32,128]{2,0,1:T(8,128)S(1)}, f32[64,32,128]{2,0,1:T(8,128)S(1)}) fusion(f32[64,32,128]{2,1,0:T(8,128)} %collective-permute-done.2, f32[64,32,128]{2,1,0:T(8,128)} %copy-done.3, pred[]{:T(512)S(6)} %eq.17), kind=kLoop, calls=%fused_computation.28 | loop fusion | flops 524288 | bytes 4194305 | tf_op jit(solution)/shard_map/jit(_where)/select_n | solution.py:196
  192.6 2.2 fusion.19
  195.0 0.9 fusion.18
  195.9 2.5 %copy.57 = f32[128,32,128]{2,1,0:T(8,128)} copy(f32[128,32,128]{2,0,1:T(8,128)S(1)} %get-tuple-element.20) | data formatting | bytes 4194304 | tf_op jit(solution)/shard_map/concatenate | solution.py:195
  198.5 2.7 %reshape.69 = f32[128,4096,1]{1,0,2:T(8,128)} reshape(f32[128,32,128]{2,1,0:T(8,128)} %copy.57) | data formatting | bytes 4194304 | tf_op jit(solution)/shard_map/reshape | solution.py:199
  201.3 5.0 %fusion.15 = f32[2,128,128]{1,2,0:T(8,128)S(1)} fusion(f32[2,128,128]{1,2,0:T(8,128)S(1)} %copy-done.13, f32[128,4096,1]{1,0,2:T(8,128)} %reshape.69, f32[1,1,2,4096,128]{4,3,2,1,0:T(8,128)} %param.20), kind=kOutput, calls=%fused_computation.19 | convolution fusion | flops 1610645504 | bytes 6553600 | tf_op jit(solution)/shard_map/mkb,rk->mbr/dot_general | solution.py:20
  207.8 0.8 copy.60
  208.6 0.8 copy.61
  209.4 1.6 copy.62
  211.0 0.8 fusion.45
  (67 shorter events, 5.4 us)
Async XLA Ops:
  7.2 31.3 %copy-start = (f32[1,1,4096,128]{3,2,1,0:T(8,128)S(1)}, f32[1,1,4096,128]{3,2,1,0:T(8,128)}, u32[]{:S(2)}) copy-start(f32[1,1,4096,128]{3,2,1,0:T(8,128)} %param.22) | copy-start | bytes 6291460
  7.2 1.4 copy-start.20
  7.2 3.1 %copy-start.18 = (f32[1,128,128]{2,1,0:T(8,128)S(1)}, f32[1,128,128]{2,1,0:T(8,128)}, u32[]{:S(2)}) copy-start(f32[1,128,128]{2,1,0:T(8,128)} %param.24) | copy-start | bytes 196612
  7.2 132.4 %all-gather.3.cloned.1.call-start = ((), (), s32[]{:S(2)}) async-start(), calls=%async_computation.2 | async-start | bytes 31703040 | tf_op jit(solution)/shard_map/all_gather | solution.py:165
  8.8 18.6 %copy-start.4 = (f32[1,1,4,128,128]{4,3,2,1,0:T(8,128)S(1)}, f32[1,1,4,128,128]{4,3,2,1,0:T(8,128)}, u32[]{:S(2)}) copy-start(f32[1,1,4,128,128]{4,3,2,1,0:T(8,128)} %param.14) | copy-start | bytes 786436
  8.8 19.9 %copy-start.6 = (f32[1,1,4,128,128]{4,3,2,1,0:T(8,128)S(1)}, f32[1,1,4,128,128]{4,3,2,1,0:T(8,128)}, u32[]{:S(2)}) copy-start(f32[1,1,4,128,128]{4,3,2,1,0:T(8,128)} %param.15) | copy-start | bytes 786436
  8.8 14.9 %collective-permute-start.1 = (f32[14,32,128]{2,0,1:T(8,128)S(1)}, f32[14,32,128]{2,0,1:T(8,128)}, u32[]{:S(2)}, u32[]{:S(2)}) collective-permute-start(f32[14,32,128]{2,0,1:T(8,128)S(1)} %dynamic-slice_bitcast_fusion.1), channel_id=1, source_target_pairs={{31,0},{30,1},{29,2},{28,3},{27,4},{26,5},{25,6},{24,7},{23,8},{22... | collective-permute-start | bytes 688136 | tf_op jit(solution)/shard_map/ppermute | solution.py:129
  10.4 15.2 %copy-start.17 = (f32[1,1,2,128,128]{4,3,2,1,0:T(8,128)S(1)}, f32[1,1,2,128,128]{4,3,2,1,0:T(8,128)}, u32[]{:S(2)}) copy-start(f32[1,1,2,128,128]{4,3,2,1,0:T(8,128)} %param.19) | copy-start | bytes 393220
  24.8 5.8 %copy-start.11 = (f32[1,1,2,128,128]{4,3,2,1,0:T(8,128)S(1)}, f32[1,1,2,128,128]{4,3,2,1,0:T(8,128)}, u32[]{:S(2)}) copy-start(f32[1,1,2,128,128]{4,3,2,1,0:T(8,128)} %param.18) | copy-start | bytes 393220
  24.8 6.9 %copy-start.15 = (f32[1,1,128,128]{3,2,1,0:T(8,128)S(1)}, f32[1,1,128,128]{3,2,1,0:T(8,128)}, u32[]{:S(2)}) copy-start(f32[1,1,128,128]{3,2,1,0:T(8,128)} %param.21) | copy-start | bytes 196612
  32.0 6.5 %copy-start.8 = (f32[128,128]{1,0:T(8,128)}, f32[128,128]{1,0:T(8,128)S(1)}, u32[]{:S(2)}) copy-start(f32[128,128]{1,0:T(8,128)S(1)} %fusion.43) | copy-start | bytes 196612
  40.5 1.7 copy-start.19
  44.3 1.3 copy-start.2
  45.7 2.9 %collective-permute-start = (f32[64,32,128]{2,1,0:T(8,128)S(1)}, f32[64,32,128]{2,1,0:T(8,128)}, u32[]{:S(2)}, u32[]{:S(2)}) collective-permute-start(f32[64,32,128]{2,1,0:T(8,128)S(1)} %constant_dynamic-slice_fusion.1), channel_id=1, source_target_pairs={{0,1},{1,0},{2,3},{3,2},{4,5},{5,4},{6,7},{7,6},{8,9},{9,8},{10,11... | collective-permute-start | bytes 3145736 | tf_op jit(solution)/shard_map/ppermute | solution.py:137
  184.5 2.0 copy-start.3
  184.5 4.4 %collective-permute-start.2 = (f32[64,32,128]{2,1,0:T(8,128)S(1)}, f32[64,32,128]{2,1,0:T(8,128)}, u32[]{:S(2)}, u32[]{:S(2)}) collective-permute-start(f32[64,32,128]{2,1,0:T(8,128)S(1)} %all_to_all.11), channel_id=1, source_target_pairs={{0,1},{1,0},{2,3},{3,2},{4,5},{5,4},{6,7},{7,6},{8,9},{9,8},{10,11... | collective-permute-start | bytes 3145736 | tf_op jit(solution)/shard_map/ppermute | solution.py:137
  191.6 1.0 copy-start.1
  191.6 1.0 copy-start.9
  192.6 2.2 copy-start.16
  192.6 2.4 %copy-start.12 = (f32[1,1,2,128,128]{4,3,2,1,0:T(8,128)S(1)}, f32[1,1,2,128,128]{4,3,2,1,0:T(8,128)}, u32[]{:S(2)}) copy-start(f32[1,1,2,128,128]{4,3,2,1,0:T(8,128)} %param.18) | copy-start | bytes 393220
  195.0 0.9 copy-start.10
  198.5 2.8 %copy-start.13 = (f32[2,128,128]{1,2,0:T(8,128)S(1)}, f32[2,128,128]{1,2,0:T(8,128)}, u32[]{:S(2)}) copy-start(f32[2,128,128]{1,2,0:T(8,128)} %fusion.18) | copy-start | bytes 393220
  201.2 5.0 %copy-start.14 = (f32[1,1,2,128,128]{4,3,2,1,0:T(8,128)S(1)}, f32[1,1,2,128,128]{4,3,2,1,0:T(8,128)}, u32[]{:S(2)}) copy-start(f32[1,1,2,128,128]{4,3,2,1,0:T(8,128)} %param.17) | copy-start | bytes 393220
  201.2 5.3 %copy-start.7 = (f32[1,1,4,128,128]{4,3,2,1,0:T(8,128)S(1)}, f32[1,1,4,128,128]{4,3,2,1,0:T(8,128)}, u32[]{:S(2)}) copy-start(f32[1,1,4,128,128]{4,3,2,1,0:T(8,128)} %param.15) | copy-start | bytes 786436
  201.2 5.9 %copy-start.5 = (f32[1,1,4,128,128]{4,3,2,1,0:T(8,128)S(1)}, f32[1,1,4,128,128]{4,3,2,1,0:T(8,128)}, u32[]{:S(2)}) copy-start(f32[1,1,4,128,128]{4,3,2,1,0:T(8,128)} %param.14) | copy-start | bytes 786436
Sparse Core Ops, SparseCore 0:
  25.7 113.8 all-gather.2

commit v3 on v2

--- a/solution.py
+++ b/solution.py
@@ -22,7 +22,7 @@
     )
 
 
-def sweep_kernel(rhs_ref, factor_hbm, out_ref, factor, forward, pulled, sems):
+def sweep_kernel(rhs_ref, factor_hbm, out_ref, factor, forward, pulled, sums, sems):
     layers = factor_hbm.shape[0] // KTOP
     part = BLOCK // layers
     copies = [
@@ -47,58 +47,58 @@
     def tall(row):
         return jnp.concatenate([row] * (BLOCK // 8), axis=0)
 
-    for i in range(KTOP):
+    def add(j, acc, d, shift):
+        return acc + factor[d, j - shift] * tall(forward[j])
+
+    def pull(j, carry, d, shift, wide):
+        terms = factor[d, j - shift] * wide
+        pulled[j] += jnp.sum(terms.reshape(BLOCK // 8, 8, BLOCK), axis=0)
+        return carry
+
+    def over_row(i, step, carry, unroll):
         g = i // SPAN
-        for copy in copies[i]:
-            copy.wait()
-        row = jnp.broadcast_to(rhs_ref[pl.ds(i, 1), :], (8, BLOCK))
-        acc = jnp.where(eye, tall(row), 0.0)
-
-        def add(j, acc, d, shift):
-            return acc + factor[d, j - shift] * tall(forward[j])
-
         count = min(SPAN * g, KEEP)
         if count:
-            acc = lax.fori_loop(
-                0, count, functools.partial(add, d=i, shift=0), acc, unroll=2
+            body = functools.partial(step, d=i, shift=0)
+            carry = lax.fori_loop(0, count, body, carry, unroll=unroll)
+        if SPAN * g > KEEP:
+            body = functools.partial(step, d=KTOP - 1 - i, shift=SPAN * g - KEEP)
+            carry = lax.fori_loop(KEEP, SPAN * g, body, carry, unroll=unroll)
+        return carry
+
+    for g in range(GROUPS):
+        rows = range(SPAN * g, SPAN * (g + 1))
+        for i in rows:
+            for copy in copies[i]:
+                copy.wait()
+            row = jnp.broadcast_to(rhs_ref[pl.ds(i, 1), :], (8, BLOCK))
+            start = jnp.where(eye, tall(row), 0.0)
+            sums[i % SPAN] = over_row(i, add, start, 2)
+        residuals = [-jnp.sum(sums[i % SPAN], axis=1, keepdims=True) for i in rows]
+        for i, column in zip(rows, residuals):
+            forward[i] = fold(factor[i, KEEP] * column)
+
+    pulled[...] = jnp.zeros_like(pulled)
+    for g in range(GROUPS - 1, -1, -1):
+        rows = range(SPAN * g, SPAN * (g + 1))
+        inputs = [
+            forward[i]
+            - jnp.broadcast_to(jnp.sum(pulled[i], axis=0, keepdims=True), (8, BLOCK))
+            for i in rows
+        ]
+        solved = [
+            jnp.sum(factor[i, KEEP] * tall(row), axis=1, keepdims=True)
+            for i, row in zip(rows, inputs)
+        ]
+        for i, column in zip(rows, solved):
+            wide = jnp.broadcast_to(column, (BLOCK, BLOCK))
+            sums[i % SPAN] = wide
+            out_ref[pl.ds(i, 1), :] = jnp.sum(
+                jnp.where(eye, wide, 0.0), axis=0, keepdims=True
             )
-        if SPAN * g > KEEP:
-            acc = lax.fori_loop(
-                KEEP,
-                SPAN * g,
-                functools.partial(add, d=KTOP - 1 - i, shift=SPAN * g - KEEP),
-                acc,
-                unroll=2,
-            )
-        column = jnp.sum(acc, axis=1, keepdims=True)
-        forward[i] = fold(factor[i, KEEP] * -column)
-
-    pulled[...] = jnp.zeros_like(pulled)
-    for i in range(KTOP - 1, -1, -1):
-        g = i // SPAN
-        row = forward[i] - jnp.broadcast_to(
-            jnp.sum(pulled[i], axis=0, keepdims=True), (8, BLOCK)
-        )
-        column = jnp.sum(factor[i, KEEP] * tall(row), axis=1, keepdims=True)
-        wide = jnp.broadcast_to(column, (BLOCK, BLOCK))
-        out_ref[pl.ds(i, 1), :] = jnp.sum(jnp.where(eye, wide, 0.0), axis=0, keepdims=True)
-
-        def pull(j, carry, d, shift):
-            terms = factor[d, j - shift] * wide
-            pulled[j] += jnp.sum(terms.reshape(BLOCK // 8, 8, BLOCK), axis=0)
-            return carry
-
-        count = min(SPAN * g, KEEP)
-        if count:
-            lax.fori_loop(0, count, functools.partial(pull, d=i, shift=0), 0, unroll=2)
-        if SPAN * g > KEEP:
-            lax.fori_loop(
-                KEEP,
-                SPAN * g,
-                functools.partial(pull, d=KTOP - 1 - i, shift=SPAN * g - KEEP),
-                0,
-                unroll=2,
-            )
+        for i in rows:
+            if g:
+                over_row(i, functools.partial(pull, wide=sums[i % SPAN]), 0, 2)
 
 
 def sweep(rhs, factor):
@@ -111,10 +111,124 @@
             pltpu.VMEM((KTOP, SLOTS, BLOCK, BLOCK), jnp.float32),
             pltpu.VMEM((KTOP, 8, BLOCK), jnp.float32),
             pltpu.VMEM((KTOP, 8, BLOCK), jnp.float32),
+            pltpu.VMEM((SPAN, BLOCK, BLOCK), jnp.float32),
             pltpu.SemaphoreType.DMA((KTOP, factor.shape[0] // KTOP)),
         ],
         compiler_params=pltpu.CompilerParams(vmem_limit_bytes=44 * 2**20),
     )(rhs, factor)
+
+
+def split(value):
+    high = value.astype(jnp.bfloat16)
+    return high, (value - high.astype(jnp.float32)).astype(jnp.bfloat16)
+
+
+def dot3(left, right):
+    (a, b), (c, d) = left, right
+    dot = functools.partial(jnp.dot, preferred_element_type=jnp.float32)
+    return dot(a, c) + (dot(a, d) + dot(b, c))
+
+
+def finish_kernel(
+    place_ref,
+    near_ref,
+    far_ref,
+    root_panel_ref,
+    mid_panel_ref,
+    forward_root_ref,
+    forward_mid_ref,
+    forward_leaf_ref,
+    root_inverse_ref,
+    mid_inverse_ref,
+    mid_coupling_ref,
+    leaf_inverse_ref,
+    leaf_coupling_ref,
+    leaf_out,
+    mid_out,
+    root_out,
+    top_out,
+    acc,
+):
+    step = pl.program_id(0)
+    half = near_ref.shape[0] // KTOP
+    blocks = root_panel_ref.shape[0] // BLOCK
+    mids = mid_panel_ref.shape[0]
+    leaves = leaf_inverse_ref.shape[0]
+    core = place_ref[1]
+
+    def columns_of(block):
+        return jnp.concatenate(
+            [
+                near_ref[pl.ds(block, half, stride=KTOP), :],
+                far_ref[pl.ds(block, half, stride=KTOP), :],
+            ],
+            axis=0,
+        )
+
+    def ordered(value):
+        return jnp.where(
+            core == 0, value, jnp.concatenate([value[half:], value[:half]], axis=0)
+        )
+
+    @pl.when(step == 0)
+    def _():
+        acc[...] = jnp.zeros_like(acc)
+
+    solved = split(
+        jnp.concatenate([columns_of(step * blocks + t) for t in range(blocks)], axis=1)
+    )
+    acc[0] += dot3(solved, split(root_panel_ref[...]))
+    for m in range(mids):
+        acc[1 + m] += dot3(solved, split(mid_panel_ref[m]))
+
+    @pl.when(step == pl.num_programs(0) - 1)
+    def _():
+        top_out[...] = ordered(columns_of(place_ref[0])).T
+        pulls = [ordered(acc[n]).T for n in range(1 + mids)]
+        root = dot3(split(root_inverse_ref[...]), split(forward_root_ref[...] - pulls[0]))
+        root_out[...] = root
+        root = split(root)
+        for m in range(mids):
+            term = dot3(split(mid_coupling_ref[m]), root)
+            mid = dot3(
+                split(mid_inverse_ref[m]), split(forward_mid_ref[m] - term - pulls[1 + m])
+            )
+            mid_out[m] = mid
+            mid = split(mid)
+            for p in range(m * leaves // mids, (m + 1) * leaves // mids):
+                term = dot3(split(leaf_coupling_ref[p]), mid)
+                leaf_out[p] = dot3(
+                    split(leaf_inverse_ref[p]), split(forward_leaf_ref[p] - term)
+                )
+
+
+def finish(place, near, far, root_panel, mid_panel, *small):
+    mids, leaves = mid_panel.shape[0], small[2].shape[0]
+    steps = 8
+    rows = KTOP * BLOCK // steps
+    whole = pl.BlockSpec(memory_space=pltpu.VMEM)
+    out = functools.partial(jax.ShapeDtypeStruct, dtype=jnp.float32)
+    return pl.pallas_call(
+        finish_kernel,
+        grid=(steps,),
+        out_shape=(
+            out((leaves, BLOCK, BLOCK)),
+            out((mids, BLOCK, BLOCK)),
+            out((BLOCK, BLOCK)),
+            out((BLOCK, BLOCK)),
+        ),
+        in_specs=[
+            pl.BlockSpec(memory_space=pltpu.SMEM),
+            whole,
+            whole,
+            pl.BlockSpec((rows, BLOCK), lambda t: (t, 0)),
+            pl.BlockSpec((mids, rows, BLOCK), lambda t: (0, t, 0)),
+        ]
+        + [whole] * len(small),
+        out_specs=(whole,) * 4,
+        scratch_shapes=[pltpu.VMEM((1 + mids, BLOCK, BLOCK), jnp.float32)],
+        compiler_params=pltpu.CompilerParams(vmem_limit_bytes=40 * 2**20),
+    )(place, near, far, root_panel, mid_panel, *small)
 
 
 def pack_rows(factor_row, pattern_row, inverse, position, layer, layers):
@@ -192,22 +306,20 @@
     everywhere = jnp.broadcast_to(own_column[None], (half, KTOP, BLOCK))
     near = lax.all_to_all(everywhere, ("layer", "chip"), 0, 0, tiled=True)
     far = swap_cores(near)
-    solved = jnp.concatenate(
-        [jnp.where(core == 0, near, far), jnp.where(core == 0, far, near)], axis=0
-    )
-    own_top = lax.dynamic_index_in_dim(solved, position, 1, keepdims=False).T
-    flat = solved.reshape(columns, KTOP * BLOCK)
-    root_pull = product("kb,rk->br", root_panel, flat)
-    mid_pull = product("mkb,rk->mbr", mid_panel, flat)
-    back_root = product("ba,br->ar", root_inverse[0, 0], forward_root - root_pull)
-    back_mid = product(
-        "mba,mbr->mar",
-        mid_inverse[0, 0],
-        forward_mid - product("mab,ar->mbr", mid_coupling[0, 0], back_root) - mid_pull,
-    )
-    parent = jnp.repeat(back_mid, 2, axis=0)
-    back_leaf = product(
-        "pba,pbr->par", leaf_inv, forward_leaf - product("pab,par->pbr", leaf_links, parent)
+    back_leaf, back_mid, back_root, own_top = finish(
+        jnp.stack([position, core]).astype(jnp.int32),
+        near.reshape(half * KTOP, BLOCK),
+        far.reshape(half * KTOP, BLOCK),
+        root_panel,
+        mid_panel,
+        forward_root,
+        forward_mid,
+        forward_leaf,
+        root_inverse[0, 0].T,
+        mid_inverse[0, 0].transpose(0, 2, 1),
+        mid_coupling[0, 0].transpose(0, 2, 1),
+        leaf_inv.transpose(0, 2, 1),
+        leaf_links.transpose(0, 2, 1),
     )
     return (back_leaf[None, None], back_mid[None, None], back_root[None, None], own_top[None])
 

time: 220 us -> 221 us (level)
  matrix products: 22.8 us -> 12.7 us
  local copies, waits for them, and re-layouts: 16.9 us -> 26.1 us
  Pallas kernels: 19.2 us -> 26.1 us
  other arithmetic: 9.02 us -> 5.23 us
    unnamed x52 -> x51, local copies, waits for them, and re-layouts: 10.5 us -> 23.4 us
    dot_general x14 -> x7, matrix products: 22.8 us -> 12.7 us  [product(): jnp.einsum(spec, left, right, precision=lax.Precision.HIGHEST, preferred_...]
    pallas_call x0 -> x1, Pallas kernels: none -> 8.79 us  [finish(): pl.pallas_call(finish_kernel, grid=(steps,), out_shape=(out((leaves, BLOC...]
    reshape x1 -> x0, local copies, waits for them, and re-layouts: 2.75 us -> none  [local(): flat = solved.reshape(columns, KTOP * BLOCK)]
    select_n x1 -> x0, other arithmetic: 2.69 us -> none  [local(): jnp.where(core == 0, near, far)]
    concatenate x1 -> x0, local copies, waits for them, and re-layouts: 2.54 us -> none  [local(): jnp.concatenate([jnp.where(core == 0, near, far), jnp.where(core == 0, fa...]
    ppermute x2, waiting for transfers between devices: 5.19 us -> 2.78 us  [swap_cores(): return lax.ppermute(value, 'core', [(0, 1), (1, 0)])]
  transfers between devices with their start and end apart: 4 -> 4, of which waited for: 4 -> 3; matrix products, arithmetic and copies ran while one was open for 9% -> 13% of each run, Pallas kernels for 0% -> 0%
where the time goes in v3:
time: 221 us; the launch traced here: 220 us
  waiting for transfers between devices  72.3 us (33%)
  blocking collectives  59.7 us (27%)
  local copies, waits for them, and re-layouts  26.1 us (12%)
  Pallas kernels  26.1 us (12%)
  between operations  14.4 us (7%)
  matrix products  12.7 us (6%)
  other arithmetic  5.23 us (2%)
  starting transfers between devices  3.57 us (2%)
    all_gather x1, waiting for transfers between devices, local(): factor = lax.all_gather(packed, ('layer',) + GRID, axis=0)  56.2 us
    all_to_all x1, blocking collectives, local(): lax.all_to_all(home + swap_cores(away), ('layer', 'chip'), 0, 0, tiled=True)  34.1 us
    all_to_all x1, blocking collectives, local(): near = lax.all_to_all(everywhere, ('layer', 'chip'), 0, 0, tiled=True)  25.6 us
    unnamed x51, local copies, waits for them, and re-layouts  23.4 us
    pallas_call x1, Pallas kernels, sweep(): pl.pallas_call(sweep_kernel, out_shape=jax.ShapeDtypeStruct((KTOP, BLOCK)...  17.3 us
    ppermute x1, waiting for transfers between devices, pack_rows(): lax.ppermute(excess, GRID, [(KTOP - 1 - d, d) for d in range(KTOP // 2)])  13.3 us
    dot_general x7, matrix products, product(): jnp.einsum(spec, left, right, precision=lax.Precision.HIGHEST, preferred_...  12.7 us
    pallas_call x1, Pallas kernels, finish(): pl.pallas_call(finish_kernel, grid=(steps,), out_shape=(out((leaves, BLOC...  8.79 us
  transfers between devices with their start and end apart: 4, of which 3 were waited for; matrix products, arithmetic and copies ran while one was open for 13% of the time, Pallas kernels for 0%

profile of v3, /device:TPU:1, one launch (start us, length us, event | category | flops | bytes accessed | tf_op | source)
XLA Modules:
  0.0 220.0 jit_solution(3849559191233742690)
XLA Ops:
  7.3 1.5 copy-done
  9.2 1.4 collective-permute-start.1
  10.7 13.3 %collective-permute-done.1 = f32[14,32,128]{2,0,1:T(8,128)} collective-permute-done((f32[14,32,128]{2,0,1:T(8,128)S(1)}, f32[14,32,128]{2,0,1:T(8,128)}, u32[]{:S(2)}, u32[]{:S(2)}) %collective-permute-start.1) | collective-permute-done | bytes 229408 | tf_op jit(solution)/shard_map/ppermute | solution.py:243
  24.0 1.1 slice_select_fusion
  26.1 0.9 copy.48
  27.0 1.3 fusion.6.forward_leaf_ref
  29.0 1.3 convolution_bitcast_fusion.1.forward_mid_ref
  31.0 6.8 %convolution_bitcast_fusion = f32[128,4096]{1,0:T(8,128)S(1)} fusion(f32[2,128,128]{2,1,0:T(8,128)S(1)} %convolution_bitcast_fusion.1.forward_mid_ref, f32[1,1,2,4096,128]{4,3,2,1,0:T(8,128)} %param.20), kind=kOutput, calls=%fused_computation | convolution fusion | flops 1610612736 | bytes 6422528 | tf_op jit(solution)/shard_map/mbr,mkb->rk/dot_general | solution.py:20
  37.9 2.0 fusion
  39.9 1.7 copy.84
  41.6 2.0 bitcast_subtract_fusion
  43.7 1.3 copy-done.10
  45.2 2.8 %collective-permute-done = f32[64,32,128]{2,1,0:T(8,128)} collective-permute-done((f32[64,32,128]{2,1,0:T(8,128)S(1)}, f32[64,32,128]{2,1,0:T(8,128)}, u32[]{:S(2)}, u32[]{:S(2)}) %collective-permute-start) | collective-permute-done | bytes 1048608 | tf_op jit(solution)/shard_map/ppermute | solution.py:251
  47.9 1.7 dynamic-slice_add_fusion
  49.7 34.1 %all_to_all.10 = f32[64,32,128]{2,1,0:T(8,128)S(1)} all-to-all(f32[64,32,128]{2,1,0:T(8,128)S(1)} %dynamic-slice_add_fusion), channel_id=1, replica_groups=mesh['layer'=4,'chip'=16,'core'=2] {'layer','chip'}, dimensions={0} | all-to-all | bytes 2097152 | tf_op jit(solution)/shard_map/all_to_all | solution.py:302
  83.9 56.2 %all-gather.3.cloned.1.call-done = f32[1920,32,128]{2,1,0:T(8,128)} async-done(((f32[15,32,128]{2,1,0:T(8,128)}), f32[1920,32,128]{2,1,0:T(8,128)}) %all-gather.3.cloned.1.call-update) | async-done | bytes 31457296 | tf_op jit(solution)/shard_map/all_gather | solution.py:279
  140.1 17.3 %shard_map.165 = f32[32,128]{1,0:T(8,128)S(1)} custom-call(f32[32,128]{1,0:T(8,128)S(1)} %reduce_sum.19.rhs_ref, f32[128,15,32,128]{3,2,1,0:T(8,128)} %bitcast.106), custom_call_target="tpu_custom_call" | custom-call | tf_op jit(solution)/shard_map/pallas_call | solution.py:105
  157.5 25.6 %all_to_all.11 = f32[64,32,128]{2,1,0:T(8,128)S(1)} all-to-all(f32[64,32,128]{2,1,0:T(8,128)S(1)} %broadcast_in_dim.60), channel_id=1, replica_groups=mesh['layer'=4,'chip'=16,'core'=2] {'layer','chip'}, dimensions={0} | all-to-all | bytes 2097152 | tf_op jit(solution)/shard_map/all_to_all | solution.py:307
  183.0 2.0 collective-permute-start.2
  185.1 1.6 copy.66
  186.6 1.6 copy.61
  188.2 1.7 copy.55
  189.9 1.7 copy.58
  191.5 1.8 copy.50
  193.3 1.8 copy.52
  195.2 2.2 copy-done.1
  197.4 1.6 copy-done.3
  199.0 0.9 copy-done.4
  199.9 0.9 copy-done.5
  200.9 0.9 copy-done.6
  201.8 0.9 copy-done.7
  204.3 8.8 %shard_map.166 = (f32[4,128,128]{2,1,0:T(8,128)}, f32[2,128,128]{2,1,0:T(8,128)}, f32[128,128]{1,0:T(8,128)}, f32[128,128]{1,0:T(8,128)}) custom-call(s32[2]{0:T(128)S(1)} %pad_add_fusion.place_ref, f32[2048,128]{1,0:T(8,128)S(1)} %bitcast.99, f32[2048,128]{1,0:T(8,128)} %bitcast.32.far_ref, f32[4096,128]{1,0:T(8,128)S(1)} %bitcast.98, ...), custom_call_target="tpu_custom_call" | custom-call | tf_op jit(solution)/shard_map/pallas_call | solution.py:211
  (56 shorter events, 4.9 us)
Async XLA Ops:
  7.2 1.6 copy-start
  7.2 1.7 copy-start.19
  7.2 3.4 %copy-start.17 = (f32[1,128,128]{2,1,0:T(8,128)S(1)}, f32[1,128,128]{2,1,0:T(8,128)}, u32[]{:S(2)}) copy-start(f32[1,128,128]{2,1,0:T(8,128)} %param.24) | copy-start | bytes 196612
  7.2 132.9 %all-gather.3.cloned.1.call-start = ((), (), s32[]{:S(2)}) async-start(), calls=%async_computation.2 | async-start | bytes 31703040 | tf_op jit(solution)/shard_map/all_gather | solution.py:279
  8.9 18.1 %copy-start.11 = (f32[1,1,4,128,128]{4,3,2,1,0:T(8,128)S(1)}, f32[1,1,4,128,128]{4,3,2,1,0:T(8,128)}, u32[]{:S(2)}) copy-start(f32[1,1,4,128,128]{4,3,2,1,0:T(8,128)} %param.14) | copy-start | bytes 786436
  9.1 19.3 %copy-start.12 = (f32[1,1,4,128,128]{4,3,2,1,0:T(8,128)S(1)}, f32[1,1,4,128,128]{4,3,2,1,0:T(8,128)}, u32[]{:S(2)}) copy-start(f32[1,1,4,128,128]{4,3,2,1,0:T(8,128)} %param.15) | copy-start | bytes 786436
  9.2 14.9 %collective-permute-start.1 = (f32[14,32,128]{2,0,1:T(8,128)S(1)}, f32[14,32,128]{2,0,1:T(8,128)}, u32[]{:S(2)}, u32[]{:S(2)}) collective-permute-start(f32[14,32,128]{2,0,1:T(8,128)S(1)} %dynamic-slice_bitcast_fusion.1), channel_id=1, source_target_pairs={{31,0},{30,1},{29,2},{28,3},{27,4},{26,5},{25,6},{24,7},{23,8},{22... | collective-permute-start | bytes 688136 | tf_op jit(solution)/shard_map/ppermute | solution.py:243
  24.0 2.0 copy-start.16
  24.0 6.3 %copy-start.14 = (f32[1,1,2,128,128]{4,3,2,1,0:T(8,128)S(1)}, f32[1,1,2,128,128]{4,3,2,1,0:T(8,128)}, u32[]{:S(2)}) copy-start(f32[1,1,2,128,128]{4,3,2,1,0:T(8,128)} %param.18) | copy-start | bytes 393220
  25.1 5.6 %copy-start.15 = (f32[1,1,128,128]{3,2,1,0:T(8,128)S(1)}, f32[1,1,128,128]{3,2,1,0:T(8,128)}, u32[]{:S(2)}) copy-start(f32[1,1,128,128]{3,2,1,0:T(8,128)} %param.21) | copy-start | bytes 196612
  31.0 6.9 %copy-start.13 = (f32[128,128]{1,0:T(8,128)}, f32[128,128]{1,0:T(8,128)S(1)}, u32[]{:S(2)}) copy-start(f32[128,128]{1,0:T(8,128)S(1)} %fusion.11) | copy-start | bytes 196612
  31.0 6.9 %copy-start.2 = (f32[1,1,4096,128]{3,2,1,0:T(8,128)S(1)}, f32[1,1,4096,128]{3,2,1,0:T(8,128)}, u32[]{:S(2)}) copy-start(f32[1,1,4096,128]{3,2,1,0:T(8,128)} %param.22) | copy-start | bytes 6291460
  39.8 1.7 copy-start.18
  43.7 1.3 copy-start.10
  45.1 2.9 %collective-permute-start = (f32[64,32,128]{2,1,0:T(8,128)S(1)}, f32[64,32,128]{2,1,0:T(8,128)}, u32[]{:S(2)}, u32[]{:S(2)}) collective-permute-start(f32[64,32,128]{2,1,0:T(8,128)S(1)} %constant_dynamic-slice_fusion.1), channel_id=1, source_target_pairs={{0,1},{1,0},{2,3},{3,2},{4,5},{5,4},{6,7},{7,6},{8,9},{9,8},{10,11... | collective-permute-start | bytes 3145736 | tf_op jit(solution)/shard_map/ppermute | solution.py:251
  183.0 12.1 %collective-permute-start.2 = (f32[64,32,128]{2,1,0:T(8,128)S(1)}, f32[64,32,128]{2,1,0:T(8,128)}, u32[]{:S(2)}, u32[]{:S(2)}) collective-permute-start(f32[64,32,128]{2,1,0:T(8,128)S(1)} %all_to_all.11), channel_id=1, source_target_pairs={{0,1},{1,0},{2,3},{3,2},{4,5},{5,4},{6,7},{7,6},{8,9},{9,8},{10,11... | collective-permute-start | bytes 3145736 | tf_op jit(solution)/shard_map/ppermute | solution.py:251
  195.2 2.2 copy-start.1
  197.4 1.6 copy-start.3
  199.0 0.9 copy-start.4
  199.9 0.9 copy-start.5
  200.9 0.9 copy-start.6
  201.8 0.9 copy-start.7
  202.7 0.8 copy-start.8
  203.5 0.8 copy-start.9
Sparse Core Ops, SparseCore 0:
  26.1 113.9 all-gather.2

commit v4 on v3

--- a/solution.py
+++ b/solution.py
@@ -98,7 +98,7 @@
             )
         for i in rows:
             if g:
-                over_row(i, functools.partial(pull, wide=sums[i % SPAN]), 0, 2)
+                over_row(i, functools.partial(pull, wide=sums[i % SPAN]), 0, True)
 
 
 def sweep(rhs, factor):
@@ -127,6 +127,24 @@
     (a, b), (c, d) = left, right
     dot = functools.partial(jnp.dot, preferred_element_type=jnp.float32)
     return dot(a, c) + (dot(a, d) + dot(b, c))
+
+
+def prepare_kernel(*refs):
+    outs = refs[len(refs) // 2 :]
+    for ref, out in zip(refs, outs):
+        for n in range(ref.shape[0]):
+            high, low = split(ref[n].T)
+            out[n, 0] = high
+            out[n, 1] = low
+
+
+def prepare(*matrices):
+    return pl.pallas_call(
+        prepare_kernel,
+        out_shape=tuple(
+            jax.ShapeDtypeStruct((m.shape[0], 2) + m.shape[1:], jnp.bfloat16) for m in matrices
+        ),
+    )(*matrices)
 
 
 def finish_kernel(
@@ -185,20 +203,20 @@
     def _():
         top_out[...] = ordered(columns_of(place_ref[0])).T
         pulls = [ordered(acc[n]).T for n in range(1 + mids)]
-        root = dot3(split(root_inverse_ref[...]), split(forward_root_ref[...] - pulls[0]))
+        root = dot3((root_inverse_ref[0, 0], root_inverse_ref[0, 1]), split(forward_root_ref[...] - pulls[0]))
         root_out[...] = root
         root = split(root)
         for m in range(mids):
-            term = dot3(split(mid_coupling_ref[m]), root)
+            term = dot3((mid_coupling_ref[m, 0], mid_coupling_ref[m, 1]), root)
             mid = dot3(
-                split(mid_inverse_ref[m]), split(forward_mid_ref[m] - term - pulls[1 + m])
+                (mid_inverse_ref[m, 0], mid_inverse_ref[m, 1]), split(forward_mid_ref[m] - term - pulls[1 + m])
             )
             mid_out[m] = mid
             mid = split(mid)
             for p in range(m * leaves // mids, (m + 1) * leaves // mids):
-                term = dot3(split(leaf_coupling_ref[p]), mid)
+                term = dot3((leaf_coupling_ref[p, 0], leaf_coupling_ref[p, 1]), mid)
                 leaf_out[p] = dot3(
-                    split(leaf_inverse_ref[p]), split(forward_leaf_ref[p] - term)
+                    (leaf_inverse_ref[p, 0], leaf_inverse_ref[p, 1]), split(forward_leaf_ref[p] - term)
                 )
 
 
@@ -206,28 +224,32 @@
     mids, leaves = mid_panel.shape[0], small[2].shape[0]
     steps = 8
     rows = KTOP * BLOCK // steps
-    whole = pl.BlockSpec(memory_space=pltpu.VMEM)
+
+    def whole(value):
+        return pl.BlockSpec(value.shape, lambda t: (0,) * len(value.shape))
+
     out = functools.partial(jax.ShapeDtypeStruct, dtype=jnp.float32)
+    shapes = (
+        out((leaves, BLOCK, BLOCK)),
+        out((mids, BLOCK, BLOCK)),
+        out((BLOCK, BLOCK)),
+        out((BLOCK, BLOCK)),
+    )
     return pl.pallas_call(
         finish_kernel,
         grid=(steps,),
-        out_shape=(
-            out((leaves, BLOCK, BLOCK)),
-            out((mids, BLOCK, BLOCK)),
-            out((BLOCK, BLOCK)),
-            out((BLOCK, BLOCK)),
-        ),
+        out_shape=shapes,
         in_specs=[
             pl.BlockSpec(memory_space=pltpu.SMEM),
-            whole,
-            whole,
+            whole(near),
+            whole(far),
             pl.BlockSpec((rows, BLOCK), lambda t: (t, 0)),
             pl.BlockSpec((mids, rows, BLOCK), lambda t: (0, t, 0)),
         ]
-        + [whole] * len(small),
-        out_specs=(whole,) * 4,
+        + [whole(value) for value in small],
+        out_specs=tuple(whole(value) for value in shapes),
         scratch_shapes=[pltpu.VMEM((1 + mids, BLOCK, BLOCK), jnp.float32)],
-        compiler_params=pltpu.CompilerParams(vmem_limit_bytes=40 * 2**20),
+        compiler_params=pltpu.CompilerParams(vmem_limit_bytes=60 * 2**20),
     )(place, near, far, root_panel, mid_panel, *small)
 
 
@@ -297,6 +319,10 @@
     summed = summed.reshape(columns, KTOP, BLOCK)
     mine = ((jnp.arange(KTOP) == position) & (layer == 0))[None, :, None]
     summed = summed - jnp.where(mine, top_rhs[0].T[:, None, :], 0.0)
+    prepared = prepare(
+        root_inverse[0], mid_inverse[0, 0], mid_coupling[0, 0], leaf_inv, leaf_links
+    )
+    summed, prepared = lax.optimization_barrier((summed, prepared))
     away = lax.dynamic_slice_in_dim(summed, (1 - core) * half, half)
     home = lax.dynamic_slice_in_dim(summed, core * half, half)
     parts = lax.all_to_all(home + swap_cores(away), ("layer", "chip"), 0, 0, tiled=True)
@@ -315,11 +341,7 @@
         forward_root,
         forward_mid,
         forward_leaf,
-        root_inverse[0, 0].T,
-        mid_inverse[0, 0].transpose(0, 2, 1),
-        mid_coupling[0, 0].transpose(0, 2, 1),
-        leaf_inv.transpose(0, 2, 1),
-        leaf_links.transpose(0, 2, 1),
+        *prepared,
     )
     return (back_leaf[None, None], back_mid[None, None], back_root[None, None], own_top[None])
 

time: 221 us -> 203 us (0.919)
  local copies, waits for them, and re-layouts: 26.1 us -> 11.5 us
  waiting for transfers between devices: 72.3 us -> 68.3 us
    unnamed x51 -> x36, local copies, waits for them, and re-layouts: 23.4 us -> 6.22 us
    pallas_call x1 -> x2, Pallas kernels: 8.79 us -> 13.4 us  [the longest x1 11.1 us: finish(): pl.pallas_call(finish_kernel, grid=(steps,), out_shape=shapes, in_specs=[...]
    pallas_call x1, Pallas kernels: 17.3 us -> 14.1 us  [sweep(): pl.pallas_call(sweep_kernel, out_shape=jax.ShapeDtypeStruct((KTOP, BLOCK)...]
    all_gather x1, waiting for transfers between devices: 56.2 us -> 53.3 us  [local(): factor = lax.all_gather(packed, ('layer',) + GRID, axis=0)]
  transfers between devices with their start and end apart: 4 -> 4, of which waited for: 3 -> 4; matrix products, arithmetic and copies ran while one was open for 13% -> 12% of each run, Pallas kernels for 0% -> 1%
where the time goes in v4:
time: 203 us; the launch traced here: 202 us
  waiting for transfers between devices  68.3 us (34%)
  blocking collectives  59.2 us (29%)
  Pallas kernels  27.5 us (14%)
  between operations  14.4 us (7%)
  local copies, waits for them, and re-layouts  11.5 us (6%)
  matrix products  10.9 us (5%)
  other arithmetic  7.03 us (3%)
  starting transfers between devices  3.56 us (2%)
    all_gather x1, waiting for transfers between devices, local(): factor = lax.all_gather(packed, ('layer',) + GRID, axis=0)  53.3 us
    all_to_all x1, blocking collectives, local(): lax.all_to_all(home + swap_cores(away), ('layer', 'chip'), 0, 0, tiled=True)  33.6 us
    all_to_all x1, blocking collectives, local(): near = lax.all_to_all(everywhere, ('layer', 'chip'), 0, 0, tiled=True)  25.6 us
    pallas_call x1, Pallas kernels, sweep(): pl.pallas_call(sweep_kernel, out_shape=jax.ShapeDtypeStruct((KTOP, BLOCK)...  14.1 us
    ppermute x1, waiting for transfers between devices, pack_rows(): lax.ppermute(excess, GRID, [(KTOP - 1 - d, d) for d in range(KTOP // 2)])  11.2 us
    pallas_call x1, Pallas kernels, finish(): pl.pallas_call(finish_kernel, grid=(steps,), out_shape=shapes, in_specs=[...  11.1 us
    dot_general x7, matrix products, product(): jnp.einsum(spec, left, right, precision=lax.Precision.HIGHEST, preferred_...  10.9 us
    unnamed x36, local copies, waits for them, and re-layouts  6.22 us
  transfers between devices with their start and end apart: 4, of which 4 were waited for; matrix products, arithmetic and copies ran while one was open for 12% of the time, Pallas kernels for 1%

profile of v4, /device:TPU:1, one launch (start us, length us, event | category | flops | bytes accessed | tf_op | source)
XLA Modules:
  0.0 202.5 jit_solution(3539087369735076077)
XLA Ops:
  7.2 1.5 copy-done
  9.1 0.7 dynamic-slice_bitcast_fusion.1
  9.9 1.4 collective-permute-start.1
  11.3 1.6 constant_dynamic-slice_fusion
  12.8 0.9 copy.46
  13.7 11.2 %collective-permute-done.1 = f32[14,32,128]{2,0,1:T(8,128)} collective-permute-done((f32[14,32,128]{2,0,1:T(8,128)}, f32[14,32,128]{2,0,1:T(8,128)}, u32[]{:S(2)}, u32[]{:S(2)}) %collective-permute-start.1) | collective-permute-done | bytes 229408 | tf_op jit(solution)/shard_map/ppermute | solution.py:265
  24.9 1.0 slice_select_fusion
  26.0 0.8 copy.40
  26.8 1.0 copy.33
  27.9 0.9 copy.32
  28.8 0.4 fusion.2.forward_leaf_ref
  29.2 0.6 bitcast_reduce_fusion
  29.9 0.4 convolution_bitcast_fusion.1.forward_mid_ref
  30.3 0.4 fusion.1
  30.7 0.3 fusion.4
  31.0 6.9 %convolution_bitcast_fusion = f32[128,4096]{1,0:T(8,128)S(1)} fusion(f32[2,128,128]{2,1,0:T(8,128)S(1)} %convolution_bitcast_fusion.1.forward_mid_ref, f32[1,1,2,4096,128]{4,3,2,1,0:T(8,128)} %param.20), kind=kOutput, calls=%fused_computation | convolution fusion | flops 1610612736 | bytes 6422528 | tf_op jit(solution)/shard_map/mbr,mkb->rk/dot_general | solution.py:20
  37.9 2.0 fusion
  39.9 1.7 copy.47
  41.7 2.3 %shard_map.165 = (bf16[1,2,128,128]{3,2,1,0:T(8,128)(2,1)}, bf16[2,2,128,128]{3,2,1,0:T(8,128)(2,1)}, bf16[2,2,128,128]{3,2,1,0:T(8,128)(2,1)}, bf16[4,2,128,128]{3,2,1,0:T(8,128)(2,1)}, bf16[4,2,128,128]{3,2,1,0:T(8,128)(2,1)}) custom-call(f32[1,128,128]{2,1,0:T(8,128)} %bitcast.93, f32[2,128,128]{2,1,0:T(8,128)} %bitcast.91, f32[2,128,128]{2,1,0:T(8,128)} %bitcast.90, ...), custom_call_target="tpu_custom_call" | custom-call | tf_op jit(solution)/shard_map/pallas_call | solution.py:142
  43.9 3.3 %bitcast_subtract_fusion = f32[128,32,128]{2,1,0:T(8,128)} fusion(f32[16,8,32,128]{3,2,1,0:T(8,128)} %copy.47, f32[128,128]{1,0:T(8,128)S(1)} %copy.38, pred[32]{0:T(512)(128)(4,1)S(1)} %compare_and_fusion), kind=kLoop, calls=%fused_computation.2 | loop fusion | flops 1048576 | bytes 4259872 | tf_op jit(solution)/shard_map/sub | solution.py:321
  47.3 1.3 constant_dynamic-slice_fusion.1
  48.7 2.8 %collective-permute-done = f32[64,32,128]{2,1,0:T(8,128)} collective-permute-done((f32[64,32,128]{2,1,0:T(8,128)S(1)}, f32[64,32,128]{2,1,0:T(8,128)}, u32[]{:S(2)}, u32[]{:S(2)}) %collective-permute-start) | collective-permute-done | bytes 1048608 | tf_op jit(solution)/shard_map/ppermute | solution.py:273
  51.4 1.7 dynamic-slice_add_fusion
  53.2 33.6 %all_to_all.10 = f32[64,32,128]{2,1,0:T(8,128)S(1)} all-to-all(f32[64,32,128]{2,1,0:T(8,128)S(1)} %dynamic-slice_add_fusion), channel_id=1, replica_groups=mesh['layer'=4,'chip'=16,'core'=2] {'layer','chip'}, dimensions={0} | all-to-all | bytes 2097152 | tf_op jit(solution)/shard_map/all_to_all | solution.py:328
  86.9 53.3 %all-gather.3.cloned.1.call-done = f32[1920,32,128]{2,1,0:T(8,128)} async-done(((f32[15,32,128]{2,1,0:T(8,128)}), f32[1920,32,128]{2,1,0:T(8,128)}) %all-gather.3.cloned.1.call-update) | async-done | bytes 31457296 | tf_op jit(solution)/shard_map/all_gather | solution.py:301
  140.2 14.1 %shard_map.166 = f32[32,128]{1,0:T(8,128)S(1)} custom-call(f32[32,128]{1,0:T(8,128)S(1)} %reduce_sum.19.rhs_ref, f32[128,15,32,128]{3,2,1,0:T(8,128)} %bitcast.83), custom_call_target="tpu_custom_call" | custom-call | tf_op jit(solution)/shard_map/pallas_call | solution.py:105
  154.5 25.6 %all_to_all.11 = f32[64,32,128]{2,1,0:T(8,128)S(1)} all-to-all(f32[64,32,128]{2,1,0:T(8,128)S(1)} %broadcast_in_dim.60), channel_id=1, replica_groups=mesh['layer'=4,'chip'=16,'core'=2] {'layer','chip'}, dimensions={0} | all-to-all | bytes 2097152 | tf_op jit(solution)/shard_map/all_to_all | solution.py:333
  180.0 2.0 %collective-permute-start.2 = (f32[64,32,128]{2,1,0:T(8,128)S(1)}, f32[64,32,128]{2,1,0:T(8,128)}, u32[]{:S(2)}, u32[]{:S(2)}) collective-permute-start(f32[64,32,128]{2,1,0:T(8,128)S(1)} %all_to_all.11), channel_id=1, source_target_pairs={{0,1},{1,0},{2,3},{3,2},{4,5},{5,4},{6,7},{7,6},{8,9},{9,8},{10,11... | collective-permute-start | bytes 3145736 | tf_op jit(solution)/shard_map/ppermute | solution.py:273
  182.1 0.7 copy.41
  182.8 0.6 pad_add_fusion.place_ref
  183.4 1.0 collective-permute-done.2
  184.5 11.1 %shard_map.167 = (f32[4,128,128]{2,1,0:T(8,128)}, f32[2,128,128]{2,1,0:T(8,128)}, f32[128,128]{1,0:T(8,128)}, f32[128,128]{1,0:T(8,128)}) custom-call(s32[2]{0:T(128)} %pad_add_fusion.place_ref, f32[2048,128]{1,0:T(8,128)} %bitcast.86, f32[2048,128]{1,0:T(8,128)} %bitcast.29.far_ref, f32[4096,128]{1,0:T(8,128)} %bitcast.85, f32[2,4096,128]{2,1,0:T(8,128)} %bitcast.84, ...), custom_call_target="tpu_custom_call" | custom-call | tf_op jit(solution)/shard_map/pallas_call | solution.py:238
  (42 shorter events, 0.8 us)
Async XLA Ops:
  7.2 1.6 copy-start
  7.2 1.7 copy-start.14
  7.2 133.0 %all-gather.3.cloned.1.call-start = ((), (), s32[]{:S(2)}) async-start(), calls=%async_computation.2 | async-start | bytes 31703040 | tf_op jit(solution)/shard_map/all_gather | solution.py:301
  8.9 19.8 %copy-start.11 = (f32[1,1,4,128,128]{4,3,2,1,0:T(8,128)S(1)}, f32[1,1,4,128,128]{4,3,2,1,0:T(8,128)}, u32[]{:S(2)}) copy-start(f32[1,1,4,128,128]{4,3,2,1,0:T(8,128)} %param.16) | copy-start | bytes 786436
  9.1 19.7 %copy-start.5 = (f32[1,1,4,128,128]{4,3,2,1,0:T(8,128)S(1)}, f32[1,1,4,128,128]{4,3,2,1,0:T(8,128)}, u32[]{:S(2)}) copy-start(f32[1,1,4,128,128]{4,3,2,1,0:T(8,128)} %param.14) | copy-start | bytes 786436
  9.1 20.1 %copy-start.6 = (f32[1,1,4,128,128]{4,3,2,1,0:T(8,128)S(1)}, f32[1,1,4,128,128]{4,3,2,1,0:T(8,128)}, u32[]{:S(2)}) copy-start(f32[1,1,4,128,128]{4,3,2,1,0:T(8,128)} %param.15) | copy-start | bytes 786436
  9.9 20.0 %copy-start.10 = (f32[1,1,2,128,128]{4,3,2,1,0:T(8,128)S(1)}, f32[1,1,2,128,128]{4,3,2,1,0:T(8,128)}, u32[]{:S(2)}) copy-start(f32[1,1,2,128,128]{4,3,2,1,0:T(8,128)} %param.17) | copy-start | bytes 393220
  9.9 15.1 %collective-permute-start.1 = (f32[14,32,128]{2,0,1:T(8,128)}, f32[14,32,128]{2,0,1:T(8,128)}, u32[]{:S(2)}, u32[]{:S(2)}) collective-permute-start(f32[14,32,128]{2,0,1:T(8,128)} %dynamic-slice_bitcast_fusion.1), channel_id=1, source_target_pairs={{31,0},{30,1},{29,2},{28,3},{27,4},{26,5},{25,6},{24,7},{23,8},{22... | collective-permute-start | bytes 688136 | tf_op jit(solution)/shard_map/ppermute | solution.py:265
  26.0 4.3 %copy-start.9 = (f32[1,1,2,128,128]{4,3,2,1,0:T(8,128)S(1)}, f32[1,1,2,128,128]{4,3,2,1,0:T(8,128)}, u32[]{:S(2)}) copy-start(f32[1,1,2,128,128]{4,3,2,1,0:T(8,128)} %param.18) | copy-start | bytes 393220
  26.0 4.7 %copy-start.12 = (f32[1,1,128,128]{3,2,1,0:T(8,128)S(1)}, f32[1,1,128,128]{3,2,1,0:T(8,128)}, u32[]{:S(2)}) copy-start(f32[1,1,128,128]{3,2,1,0:T(8,128)} %param.21) | copy-start | bytes 196612
  29.2 8.7 %copy-start.3 = (f32[4,128,128]{2,1,0:T(8,128)}, f32[4,128,128]{2,1,0:T(8,128)S(1)}, u32[]{:S(2)}) copy-start(f32[4,128,128]{2,1,0:T(8,128)S(1)} %fusion.2.forward_leaf_ref) | copy-start | bytes 786436
  30.3 7.6 %copy-start.4 = (f32[2,128,128]{2,1,0:T(8,128)}, f32[2,128,128]{2,1,0:T(8,128)S(1)}, u32[]{:S(2)}) copy-start(f32[2,128,128]{2,1,0:T(8,128)S(1)} %convolution_bitcast_fusion.1.forward_mid_ref) | copy-start | bytes 393220
  31.0 6.9 %copy-start.7 = (f32[128,128]{1,0:T(8,128)}, f32[128,128]{1,0:T(8,128)S(1)}, u32[]{:S(2)}) copy-start(f32[128,128]{1,0:T(8,128)S(1)} %fusion.4) | copy-start | bytes 196612
  31.0 7.0 %copy-start.1 = (f32[1,1,4096,128]{3,2,1,0:T(8,128)S(1)}, f32[1,1,4096,128]{3,2,1,0:T(8,128)}, u32[]{:S(2)}) copy-start(f32[1,1,4096,128]{3,2,1,0:T(8,128)} %param.22) | copy-start | bytes 6291460
  39.9 1.7 copy-start.13
  48.6 2.9 %collective-permute-start = (f32[64,32,128]{2,1,0:T(8,128)S(1)}, f32[64,32,128]{2,1,0:T(8,128)}, u32[]{:S(2)}, u32[]{:S(2)}) collective-permute-start(f32[64,32,128]{2,1,0:T(8,128)S(1)} %constant_dynamic-slice_fusion.1), channel_id=1, source_target_pairs={{0,1},{1,0},{2,3},{3,2},{4,5},{5,4},{6,7},{7,6},{8,9},{9,8},{10,11... | collective-permute-start | bytes 3145736 | tf_op jit(solution)/shard_map/ppermute | solution.py:273
  154.3 27.7 %copy-start.8 = (f32[128,128]{1,0:T(8,128)S(1)}, f32[128,128]{1,0:T(8,128)}, u32[]{:S(2)}) copy-start(f32[128,128]{1,0:T(8,128)} %copy-done.7) | copy-start | bytes 196612
  180.0 4.4 %copy-start.2 = (f32[64,32,128]{2,1,0:T(8,128)}, f32[64,32,128]{2,1,0:T(8,128)S(1)}, u32[]{:S(2)}) copy-start(f32[64,32,128]{2,1,0:T(8,128)S(1)} %all_to_all.11) | copy-start | bytes 3145732
  180.0 4.4 %collective-permute-start.2 = (f32[64,32,128]{2,1,0:T(8,128)S(1)}, f32[64,32,128]{2,1,0:T(8,128)}, u32[]{:S(2)}, u32[]{:S(2)}) collective-permute-start(f32[64,32,128]{2,1,0:T(8,128)S(1)} %all_to_all.11), channel_id=1, source_target_pairs={{0,1},{1,0},{2,3},{3,2},{4,5},{5,4},{6,7},{7,6},{8,9},{9,8},{10,11... | collective-permute-start | bytes 3145736 | tf_op jit(solution)/shard_map/ppermute | solution.py:273
Sparse Core Ops, SparseCore 0:
  27.0 113.2 all-gather.2

commit v5 on v4

--- a/solution.py
+++ b/solution.py
@@ -14,6 +14,13 @@
 BLOCK = 128
 KEEP = 14
 SLOTS = KEEP + 1
+MOVED = {
+    4: ((14, 16, 8, 6),),
+    5: ((14, 16, 8, 2), (16, 20, 12, 6)),
+    6: ((14, 24, 24, 14),),
+    7: ((14, 24, 24, 10), (24, 28, 28, 14)),
+}
+FIRST, SECOND = 10, 4
 
 
 def product(spec, left, right):
@@ -24,11 +31,10 @@
 
 def sweep_kernel(rhs_ref, factor_hbm, out_ref, factor, forward, pulled, sums, sems):
     layers = factor_hbm.shape[0] // KTOP
-    part = BLOCK // layers
     copies = [
         [
             pltpu.make_async_copy(
-                factor_hbm.at[l * KTOP + d], factor.at[d, :, pl.ds(l * part, part)], sems.at[d, l]
+                factor_hbm.at[l * KTOP + d], factor.at[l * KTOP + d], sems.at[d, l]
             )
             for l in range(layers)
         ]
@@ -41,6 +47,9 @@
         jnp.int32, (BLOCK, BLOCK), 1
     )
 
+    def block(d, slot):
+        return jnp.concatenate([factor[l * KTOP + d, slot] for l in range(layers)], axis=0)
+
     def fold(value):
         return jnp.broadcast_to(jnp.sum(value, axis=0, keepdims=True), (8, BLOCK))
 
@@ -48,10 +57,10 @@
         return jnp.concatenate([row] * (BLOCK // 8), axis=0)
 
     def add(j, acc, d, shift):
-        return acc + factor[d, j - shift] * tall(forward[j])
+        return acc + block(d, j - shift) * tall(forward[j])
 
     def pull(j, carry, d, shift, wide):
-        terms = factor[d, j - shift] * wide
+        terms = block(d, j - shift) * wide
         pulled[j] += jnp.sum(terms.reshape(BLOCK // 8, 8, BLOCK), axis=0)
         return carry
 
@@ -61,9 +70,9 @@
         if count:
             body = functools.partial(step, d=i, shift=0)
             carry = lax.fori_loop(0, count, body, carry, unroll=unroll)
-        if SPAN * g > KEEP:
-            body = functools.partial(step, d=KTOP - 1 - i, shift=SPAN * g - KEEP)
-            carry = lax.fori_loop(KEEP, SPAN * g, body, carry, unroll=unroll)
+        for first, end, back, shift in MOVED.get(g, ()):
+            body = functools.partial(step, d=i - back, shift=shift)
+            carry = lax.fori_loop(first, end, body, carry, unroll=unroll)
         return carry
 
     for g in range(GROUPS):
@@ -76,7 +85,7 @@
             sums[i % SPAN] = over_row(i, add, start, 2)
         residuals = [-jnp.sum(sums[i % SPAN], axis=1, keepdims=True) for i in rows]
         for i, column in zip(rows, residuals):
-            forward[i] = fold(factor[i, KEEP] * column)
+            forward[i] = fold(block(i, KEEP) * column)
 
     pulled[...] = jnp.zeros_like(pulled)
     for g in range(GROUPS - 1, -1, -1):
@@ -87,7 +96,7 @@
             for i in rows
         ]
         solved = [
-            jnp.sum(factor[i, KEEP] * tall(row), axis=1, keepdims=True)
+            jnp.sum(block(i, KEEP) * tall(row), axis=1, keepdims=True)
             for i, row in zip(rows, inputs)
         ]
         for i, column in zip(rows, solved):
@@ -108,7 +117,7 @@
         in_specs=[pl.BlockSpec(memory_space=pltpu.VMEM), pl.BlockSpec(memory_space=pl.ANY)],
         out_specs=pl.BlockSpec(memory_space=pltpu.VMEM),
         scratch_shapes=[
-            pltpu.VMEM((KTOP, SLOTS, BLOCK, BLOCK), jnp.float32),
+            pltpu.VMEM(factor.shape, jnp.float32),
             pltpu.VMEM((KTOP, 8, BLOCK), jnp.float32),
             pltpu.VMEM((KTOP, 8, BLOCK), jnp.float32),
             pltpu.VMEM((SPAN, BLOCK, BLOCK), jnp.float32),
@@ -253,20 +262,78 @@
     )(place, near, far, root_panel, mid_panel, *small)
 
 
-def pack_rows(factor_row, pattern_row, inverse, position, layer, layers):
+def pack_kernel(
+    pattern_ref, inverse_ref, factor_hbm, keep_ref, first_ref, second_ref, rows, turned, sem
+):
+    part = rows.shape[0]
+    layer = lax.axis_index("layer")
+    own_group = (lax.axis_index("chip") * 2 + lax.axis_index("core")) // SPAN
+    top = pl.multiple_of(layer * part, part)
+    copy = pltpu.make_async_copy(factor_hbm.at[pl.ds(top, part)], rows, sem)
+    copy.start()
+    turned[...] = inverse_ref[...].T
+    keep_ref[KEEP] = turned[pl.ds(top, part), :]
+    copy.wait()
+
+    def weighted(j):
+        weight = jnp.where(j // SPAN < own_group, pattern_ref[0, j], 0).astype(jnp.float32)
+        return rows[:, pl.ds(pl.multiple_of(j * BLOCK, BLOCK), BLOCK)] * weight
+
+    for j in range(KEEP):
+        keep_ref[j] = weighted(j)
+    for t in range(FIRST):
+        first_ref[t] = weighted(KEEP + t)
+    start = jnp.where(own_group == 7, 24, 16)
+    for t in range(SECOND):
+        second_ref[t] = weighted(start + t)
+
+
+def merge_kernel(keep_ref, first_ref, second_ref, out_ref):
+    own_group = (lax.axis_index("chip") * 2 + lax.axis_index("core")) // SPAN
+    own = SPAN * own_group
+    out_ref[KEEP] = keep_ref[KEEP]
+    for slot in range(KEEP):
+        got = first_ref[jnp.clip(slot - own, 0, FIRST - 1)]
+        if slot >= KEEP - SECOND:
+            late = own_group % 2 == 0
+            got = jnp.where(late, second_ref[slot - (KEEP - SECOND)], got)
+        out_ref[slot] = jnp.where(slot < own, keep_ref[slot], got)
+
+
+def pack_rows(factor_row, pattern_row, inverse, layers):
     part = BLOCK // layers
-    own_group = position // SPAN
-    column_groups = jnp.arange(KTOP) // SPAN
-    weights = jnp.where(column_groups < own_group, pattern_row, 0).astype(jnp.float32)
-    rows = lax.dynamic_slice_in_dim(factor_row, layer * part, part)
-    blocks = rows.reshape(part, KTOP, BLOCK).transpose(1, 0, 2) * weights[:, None, None]
-    start = jnp.maximum(SPAN * own_group - KEEP, 0)
-    excess = lax.dynamic_slice_in_dim(blocks, start, KEEP)
-    got = lax.ppermute(excess, GRID, [(KTOP - 1 - d, d) for d in range(KTOP // 2)])
-    own = (jnp.arange(KEEP) < SPAN * own_group)[:, None, None]
-    packed = jnp.where(own, blocks[:KEEP], got)
-    diagonal = lax.dynamic_slice_in_dim(inverse.T, layer * part, part)
-    return jnp.concatenate([packed, diagonal[None]], axis=0)
+    out = functools.partial(jax.ShapeDtypeStruct, dtype=jnp.float32)
+    vmem = pl.BlockSpec(memory_space=pltpu.VMEM)
+    params = pltpu.CompilerParams(vmem_limit_bytes=60 * 2**20)
+    keep, first, second = pl.pallas_call(
+        pack_kernel,
+        out_shape=(
+            out((SLOTS, part, BLOCK)),
+            out((FIRST, part, BLOCK)),
+            out((SECOND, part, BLOCK)),
+        ),
+        in_specs=[
+            pl.BlockSpec(memory_space=pltpu.SMEM),
+            vmem,
+            pl.BlockSpec(memory_space=pl.ANY),
+        ],
+        out_specs=(vmem,) * 3,
+        scratch_shapes=[
+            pltpu.VMEM((part, KTOP * BLOCK), jnp.float32),
+            pltpu.VMEM((BLOCK, BLOCK), jnp.float32),
+            pltpu.SemaphoreType.DMA,
+        ],
+        compiler_params=params,
+    )(pattern_row, inverse, factor_row)
+    moves = ([], [])
+    for g, parts in MOVED.items():
+        for move, (_, _, back, _) in zip(moves, parts):
+            move += [(i, i - back) for i in range(SPAN * g, SPAN * (g + 1))]
+    first = lax.ppermute(first, GRID, moves[0])
+    second = lax.ppermute(second, GRID, moves[1])
+    return pl.pallas_call(merge_kernel, out_shape=out((SLOTS, part, BLOCK)))(
+        keep, first, second
+    )
 
 
 def swap_cores(value):
@@ -295,9 +362,7 @@
     core = lax.axis_index("core")
     layer = lax.axis_index("layer")
     layers = lax.axis_size("layer")
-    packed = pack_rows(
-        top_factor[0], top_pattern[0], top_inverse[0], position, layer, layers
-    )
+    packed = pack_rows(top_factor[0], top_pattern, top_inverse[0], layers)
     factor = lax.all_gather(packed, ("layer",) + GRID, axis=0)
 
     leaf_inv = leaf_inverse[0, 0]
@@ -325,8 +390,9 @@
     summed, prepared = lax.optimization_barrier((summed, prepared))
     away = lax.dynamic_slice_in_dim(summed, (1 - core) * half, half)
     home = lax.dynamic_slice_in_dim(summed, core * half, half)
-    parts = lax.all_to_all(home + swap_cores(away), ("layer", "chip"), 0, 0, tiled=True)
-    residual = parts.sum(axis=0)
+    parts = lax.all_to_all(home + swap_cores(away), "layer", 0, 0, tiled=True)
+    parts = parts.reshape(layers, half // layers, KTOP, BLOCK).sum(axis=0)
+    residual = lax.all_to_all(parts, "chip", 0, 0, tiled=True).sum(axis=0)
 
     own_column = sweep(residual, factor)
     everywhere = jnp.broadcast_to(own_column[None], (half, KTOP, BLOCK))

time: 203 us -> 196 us (0.966)
  local copies, waits for them, and re-layouts: 11.5 us -> 4.61 us
  waiting for transfers between devices: 68.3 us -> 61.9 us
  Pallas kernels: 27.5 us -> 32 us
  starting transfers between devices: 3.56 us -> 6.73 us
  other arithmetic: 7.03 us -> 4.13 us
    all_gather x1, waiting for transfers between devices: 53.3 us -> 47.5 us  [local(): factor = lax.all_gather(packed, ('layer',) + GRID, axis=0)]
    pallas_call x0 -> x2, Pallas kernels: none -> 4.54 us  [the longest x1 2.78 us: pack_rows(): pl.pallas_call(pack_kernel, out_shape=(out((SLOTS, part, BLOCK)), out((FI...]
    all_to_all x1 -> x2, blocking collectives: 33.6 us -> 36.6 us  [the longest x1 26.7 us: local(): parts = lax.all_to_all(home + swap_cores(away), 'layer', 0, 0, tiled=True)]
    unnamed x36 -> x35, local copies, waits for them, and re-layouts: 6.22 us -> 3.61 us
    ppermute x1 -> x2, waiting for transfers between devices: 11.2 us -> 11 us  [the longest x1 11 us: pack_rows(): second = lax.ppermute(second, GRID, moves[1])]
  transfers between devices with their start and end apart: 4 -> 5, of which waited for: 4 -> 4; matrix products, arithmetic and copies ran while one was open for 12% -> 9% of each run, Pallas kernels for 1% -> 1%
where the time goes in v5:
time: 196 us; the launch traced here: 195 us
  waiting for transfers between devices  61.9 us (32%)
  blocking collectives  60.7 us (31%)
  Pallas kernels  32 us (16%)
  between operations  14.4 us (7%)
  matrix products  10.8 us (6%)
  starting transfers between devices  6.73 us (3%)
  local copies, waits for them, and re-layouts  4.61 us (2%)
  other arithmetic  4.13 us (2%)
    all_gather x1, waiting for transfers between devices, local(): factor = lax.all_gather(packed, ('layer',) + GRID, axis=0)  47.5 us
    all_to_all x1, blocking collectives, local(): parts = lax.all_to_all(home + swap_cores(away), 'layer', 0, 0, tiled=True)  26.7 us
    all_to_all x1, blocking collectives, local(): near = lax.all_to_all(everywhere, ('layer', 'chip'), 0, 0, tiled=True)  24.2 us
    pallas_call x1, Pallas kernels, sweep(): pl.pallas_call(sweep_kernel, out_shape=jax.ShapeDtypeStruct((KTOP, BLOCK)...  14.1 us
    pallas_call x1, Pallas kernels, finish(): pl.pallas_call(finish_kernel, grid=(steps,), out_shape=shapes, in_specs=[...  11.1 us
    ppermute x1, waiting for transfers between devices, pack_rows(): second = lax.ppermute(second, GRID, moves[1])  11 us
    dot_general x7, matrix products, product(): jnp.einsum(spec, left, right, precision=lax.Precision.HIGHEST, preferred_...  10.8 us
    all_to_all x1, blocking collectives, local(): residual = lax.all_to_all(parts, 'chip', 0, 0, tiled=True).sum(axis=0)  9.93 us
  transfers between devices with their start and end apart: 5, of which 4 were waited for; matrix products, arithmetic and copies ran while one was open for 9% of the time, Pallas kernels for 1%

profile of v5, /device:TPU:1, one launch (start us, length us, event | category | flops | bytes accessed | tf_op | source)
XLA Modules:
  0.0 195.4 jit_solution(6938081926227103265)
XLA Ops:
  7.3 2.8 %shard_map.166 = (f32[15,32,128]{2,1,0:T(8,128)}, f32[10,32,128]{2,1,0:T(8,128)}, f32[4,32,128]{2,1,0:T(8,128)}) custom-call(s32[1,32]{1,0:T(1,128)} %pattern_ref.1, f32[128,128]{1,0:T(8,128)} %bitcast.84, f32[128,4096]{1,0:T(8,128)} %bitcast.76), custom_call_target="tpu_custom_call" | custom-call | tf_op jit(solution)/shard_map/pallas_call | solution.py:308
  10.1 1.4 collective-permute-start.1
  11.5 1.3 collective-permute-start.2
  12.8 11.0 %collective-permute-done.2.second_ref = f32[4,32,128]{2,1,0:T(8,128)S(1)} collective-permute-done((f32[4,32,128]{2,1,0:T(8,128)}, f32[4,32,128]{2,1,0:T(8,128)S(1)}, u32[]{:S(2)}, u32[]{:S(2)}) %collective-permute-start.2) | collective-permute-done | bytes 65568 | tf_op jit(solution)/shard_map/ppermute | solution.py:333
  23.9 0.6 copy-done.15
  24.6 1.8 shard_map.167
  26.4 0.1 copy.31
  26.6 0.4 fusion.2.forward_leaf_ref
  27.0 0.6 bitcast_reduce_fusion
  27.6 0.4 convolution_bitcast_fusion.1.forward_mid_ref
  28.0 0.4 fusion.1
  28.4 0.3 fusion.4
  28.7 6.8 %convolution_bitcast_fusion = f32[128,4096]{1,0:T(8,128)S(1)} fusion(f32[2,128,128]{2,1,0:T(8,128)S(1)} %convolution_bitcast_fusion.1.forward_mid_ref, f32[1,1,2,4096,128]{4,3,2,1,0:T(8,128)} %param.20), kind=kOutput, calls=%fused_computation | convolution fusion | flops 1610612736 | bytes 6422528 | tf_op jit(solution)/shard_map/mbr,mkb->rk/dot_general | solution.py:27
  35.6 2.0 %fusion = f32[16,8,32,128]{3,1,2,0:T(8,128)S(1)} fusion(f32[128,4096]{1,0:T(8,128)S(1)} %convolution_bitcast_fusion, f32[128,128]{1,0:T(8,128)S(1)} %fusion.4, f32[1,1,4096,128]{3,2,1,0:T(8,128)S(1)} %copy-done.1), kind=kOutput, calls=%fused_computation.3 | convolution fusion | flops 805830656 | bytes 6356992 | tf_op jit(solution)/shard_map/br,kb->rk/dot_general | solution.py:27
  37.6 1.7 copy.42
  39.4 2.3 %shard_map.165 = (bf16[1,2,128,128]{3,2,1,0:T(8,128)(2,1)}, bf16[2,2,128,128]{3,2,1,0:T(8,128)(2,1)}, bf16[2,2,128,128]{3,2,1,0:T(8,128)(2,1)}, bf16[4,2,128,128]{3,2,1,0:T(8,128)(2,1)}, bf16[4,2,128,128]{3,2,1,0:T(8,128)(2,1)}) custom-call(f32[1,128,128]{2,1,0:T(8,128)} %bitcast.83, f32[2,128,128]{2,1,0:T(8,128)} %bitcast.81, f32[2,128,128]{2,1,0:T(8,128)} %bitcast.80, ...), custom_call_target="tpu_custom_call" | custom-call | tf_op jit(solution)/shard_map/pallas_call | solution.py:151
  41.6 2.0 %bitcast_subtract_fusion = f32[128,32,128]{2,1,0:T(8,128)S(1)} fusion(f32[16,8,32,128]{3,2,1,0:T(8,128)} %copy.42, f32[128,128]{1,0:T(8,128)S(1)} %copy.36, pred[32]{0:T(512)(128)(4,1)S(1)} %compare_and_fusion), kind=kLoop, calls=%fused_computation.2 | loop fusion | flops 1048576 | bytes 4259872 | tf_op jit(solution)/shard_map/sub | solution.py:386
  43.7 1.9 collective-permute-start
  45.7 2.4 %collective-permute-done = f32[64,32,128]{2,1,0:T(8,128)} collective-permute-done((f32[64,32,128]{2,1,0:T(8,128)S(1)}, f32[64,32,128]{2,1,0:T(8,128)}, u32[]{:S(2)}, u32[]{:S(2)}) %collective-permute-start) | collective-permute-done | bytes 1048608 | tf_op jit(solution)/shard_map/ppermute | solution.py:340
  48.1 1.4 dynamic-slice_add_fusion
  49.5 26.7 %all_to_all.15 = f32[64,32,128]{2,1,0:T(8,128)S(1)} all-to-all(f32[64,32,128]{2,1,0:T(8,128)S(1)} %dynamic-slice_add_fusion), channel_id=1, replica_groups=mesh['layer'=4,'chip'=16,'core'=2] {'layer'}, dimensions={0} | all-to-all | bytes 2097152 | tf_op jit(solution)/shard_map/all_to_all | solution.py:393
  76.3 9.9 %all_to_all.16 = f32[16,32,128]{2,1,0:T(8,128)S(1)} all-to-all(f32[16,32,128]{2,1,0:T(8,128)S(1)} %reduce_sum.28), channel_id=1, replica_groups=mesh['layer'=4,'chip'=16,'core'=2] {'chip'}, dimensions={0} | all-to-all | bytes 524288 | tf_op jit(solution)/shard_map/all_to_all | solution.py:395
  86.2 47.5 %all-gather.3.cloned.1.call-done = f32[1920,32,128]{2,1,0:T(8,128)} async-done(((f32[15,32,128]{2,1,0:T(8,128)}), f32[1920,32,128]{2,1,0:T(8,128)}) %all-gather.3.cloned.1.call-update) | async-done | bytes 31457296 | tf_op jit(solution)/shard_map/all_gather | solution.py:366
  133.7 14.1 %shard_map.168 = f32[32,128]{1,0:T(8,128)S(1)} custom-call(f32[32,128]{1,0:T(8,128)S(1)} %reduce_sum.29.rhs_ref, f32[128,15,32,128]{3,2,1,0:T(8,128)} %bitcast.71), custom_call_target="tpu_custom_call" | custom-call | tf_op jit(solution)/shard_map/pallas_call | solution.py:114
  147.8 0.1 broadcast_in_dim.43
  148.0 24.2 %all_to_all.17 = f32[64,32,128]{2,1,0:T(8,128)S(1)} all-to-all(f32[64,32,128]{2,1,0:T(8,128)S(1)} %broadcast_in_dim.43), channel_id=1, replica_groups=mesh['layer'=4,'chip'=16,'core'=2] {'layer','chip'}, dimensions={0} | all-to-all | bytes 2097152 | tf_op jit(solution)/shard_map/all_to_all | solution.py:399
  172.1 2.0 %collective-permute-start.3 = (f32[64,32,128]{2,1,0:T(8,128)S(1)}, f32[64,32,128]{2,1,0:T(8,128)S(1)}, u32[]{:S(2)}, u32[]{:S(2)}) collective-permute-start(f32[64,32,128]{2,1,0:T(8,128)S(1)} %all_to_all.17), channel_id=1, source_target_pairs={{0,1},{1,0},{2,3},{3,2},{4,5},{5,4},{6,7},{7,6},{8,9},{9,8},{10,11... | collective-permute-start | bytes 3145736 | tf_op jit(solution)/shard_map/ppermute | solution.py:340
  174.2 0.7 copy.37
  174.9 0.6 pad_add_fusion.place_ref
  175.5 1.0 collective-permute-done.3
  176.4 1.0 copy-done.5
  177.4 11.1 %shard_map.169 = (f32[4,128,128]{2,1,0:T(8,128)}, f32[2,128,128]{2,1,0:T(8,128)}, f32[128,128]{1,0:T(8,128)}, f32[128,128]{1,0:T(8,128)}) custom-call(s32[2]{0:T(128)} %pad_add_fusion.place_ref, f32[2048,128]{1,0:T(8,128)} %bitcast.74, f32[2048,128]{1,0:T(8,128)} %bitcast.77, f32[4096,128]{1,0:T(8,128)} %bitcast.73, f32[2,4096,128]{2,1,0:T(8,128)} %bitcast.72, ...), custom_call_target="tpu_custom_call" | custom-call | tf_op jit(solution)/shard_map/pallas_call | solution.py:247
  (39 shorter events, 0.6 us)
Async XLA Ops:
  7.2 19.4 %copy-start = (f32[1,1,4,128,128]{4,3,2,1,0:T(8,128)S(1)}, f32[1,1,4,128,128]{4,3,2,1,0:T(8,128)}, u32[]{:S(2)}) copy-start(f32[1,1,4,128,128]{4,3,2,1,0:T(8,128)} %param.16) | copy-start | bytes 786436
  7.2 19.2 %copy-start.12 = (f32[1,1,2,128,128]{4,3,2,1,0:T(8,128)S(1)}, f32[1,1,2,128,128]{4,3,2,1,0:T(8,128)}, u32[]{:S(2)}) copy-start(f32[1,1,2,128,128]{4,3,2,1,0:T(8,128)} %param.19) | copy-start | bytes 393220
  7.2 19.3 %copy-start.13 = (f32[1,1,128,128]{3,2,1,0:T(8,128)S(1)}, f32[1,1,128,128]{3,2,1,0:T(8,128)}, u32[]{:S(2)}) copy-start(f32[1,1,128,128]{3,2,1,0:T(8,128)} %param.23) | copy-start | bytes 196612
  7.2 19.4 %copy-start.6 = (f32[1,1,4,128,128]{4,3,2,1,0:T(8,128)S(1)}, f32[1,1,4,128,128]{4,3,2,1,0:T(8,128)}, u32[]{:S(2)}) copy-start(f32[1,1,4,128,128]{4,3,2,1,0:T(8,128)} %param.14) | copy-start | bytes 786436
  7.2 126.5 %all-gather.3.cloned.1.call-start = ((), (), s32[]{:S(2)}) async-start(), calls=%async_computation.3 | async-start | bytes 31703040 | tf_op jit(solution)/shard_map/all_gather | solution.py:366
  7.3 19.7 %copy-start.7 = (f32[1,1,4,128,128]{4,3,2,1,0:T(8,128)S(1)}, f32[1,1,4,128,128]{4,3,2,1,0:T(8,128)}, u32[]{:S(2)}) copy-start(f32[1,1,4,128,128]{4,3,2,1,0:T(8,128)} %param.15) | copy-start | bytes 786436
  7.3 20.3 %copy-start.9 = (f32[1,1,2,128,128]{4,3,2,1,0:T(8,128)S(1)}, f32[1,1,2,128,128]{4,3,2,1,0:T(8,128)}, u32[]{:S(2)}) copy-start(f32[1,1,2,128,128]{4,3,2,1,0:T(8,128)} %param.17) | copy-start | bytes 393220
  10.1 17.9 %copy-start.8 = (f32[1,1,2,128,128]{4,3,2,1,0:T(8,128)S(1)}, f32[1,1,2,128,128]{4,3,2,1,0:T(8,128)}, u32[]{:S(2)}) copy-start(f32[1,1,2,128,128]{4,3,2,1,0:T(8,128)} %param.18) | copy-start | bytes 393220
  10.1 18.3 %copy-start.10 = (f32[1,1,128,128]{3,2,1,0:T(8,128)S(1)}, f32[1,1,128,128]{3,2,1,0:T(8,128)}, u32[]{:S(2)}) copy-start(f32[1,1,128,128]{3,2,1,0:T(8,128)} %param.21) | copy-start | bytes 196612
  10.1 13.8 %collective-permute-start.1 = (f32[10,32,128]{2,1,0:T(8,128)}, f32[10,32,128]{2,1,0:T(8,128)S(1)}, u32[]{:S(2)}, u32[]{:S(2)}) collective-permute-start(f32[10,32,128]{2,1,0:T(8,128)} %get-tuple-element.29), channel_id=1, source_target_pairs={{16,8},{17,9},{18,10},{19,11},{20,12},{21,13},{22,14},{23,15},{24,... | collective-permute-start | bytes 491528 | tf_op jit(solution)/shard_map/ppermute | solution.py:332
  11.5 12.3 %collective-permute-start.2 = (f32[4,32,128]{2,1,0:T(8,128)}, f32[4,32,128]{2,1,0:T(8,128)S(1)}, u32[]{:S(2)}, u32[]{:S(2)}) collective-permute-start(f32[4,32,128]{2,1,0:T(8,128)} %get-tuple-element.30), channel_id=1, source_target_pairs={{20,8},{21,9},{22,10},{23,11},{28,0},{29,1},{30,2},{31,3},{52,40},... | collective-permute-start | bytes 196616 | tf_op jit(solution)/shard_map/ppermute | solution.py:333
  23.9 0.6 copy-start.15
  23.9 0.7 copy-start.11
  27.0 8.6 %copy-start.3 = (f32[4,128,128]{2,1,0:T(8,128)}, f32[4,128,128]{2,1,0:T(8,128)S(1)}, u32[]{:S(2)}) copy-start(f32[4,128,128]{2,1,0:T(8,128)S(1)} %fusion.2.forward_leaf_ref) | copy-start | bytes 786436
  28.0 7.5 %copy-start.4 = (f32[2,128,128]{2,1,0:T(8,128)}, f32[2,128,128]{2,1,0:T(8,128)S(1)}, u32[]{:S(2)}) copy-start(f32[2,128,128]{2,1,0:T(8,128)S(1)} %convolution_bitcast_fusion.1.forward_mid_ref) | copy-start | bytes 393220
  28.7 6.9 %copy-start.1 = (f32[1,1,4096,128]{3,2,1,0:T(8,128)S(1)}, f32[1,1,4096,128]{3,2,1,0:T(8,128)}, u32[]{:S(2)}) copy-start(f32[1,1,4096,128]{3,2,1,0:T(8,128)} %param.22) | copy-start | bytes 6291460
  37.6 1.7 copy-start.14
  43.7 4.4 %collective-permute-start = (f32[64,32,128]{2,1,0:T(8,128)S(1)}, f32[64,32,128]{2,1,0:T(8,128)}, u32[]{:S(2)}, u32[]{:S(2)}) collective-permute-start(f32[64,32,128]{2,1,0:T(8,128)S(1)} %constant_dynamic-slice_fusion), channel_id=1, source_target_pairs={{0,1},{1,0},{2,3},{3,2},{4,5},{5,4},{6,7},{7,6},{8,9},{9,8},{10,11... | collective-permute-start | bytes 3145736 | tf_op jit(solution)/shard_map/ppermute | solution.py:340
  172.1 4.3 %copy-start.2 = (f32[64,32,128]{2,1,0:T(8,128)}, f32[64,32,128]{2,1,0:T(8,128)S(1)}, u32[]{:S(2)}) copy-start(f32[64,32,128]{2,1,0:T(8,128)S(1)} %all_to_all.17) | copy-start | bytes 3145732
  172.1 4.3 %collective-permute-start.3 = (f32[64,32,128]{2,1,0:T(8,128)S(1)}, f32[64,32,128]{2,1,0:T(8,128)S(1)}, u32[]{:S(2)}, u32[]{:S(2)}) collective-permute-start(f32[64,32,128]{2,1,0:T(8,128)S(1)} %all_to_all.17), channel_id=1, source_target_pairs={{0,1},{1,0},{2,3},{3,2},{4,5},{5,4},{6,7},{7,6},{8,9},{9,8},{10,11... | collective-permute-start | bytes 3145736 | tf_op jit(solution)/shard_map/ppermute | solution.py:340
  176.4 1.0 copy-start.5
Sparse Core Ops, SparseCore 0:
  26.5 107.2 all-gather.2

commit v6 on v5

--- a/solution.py
+++ b/solution.py
@@ -12,13 +12,14 @@
 KTOP = 32
 GROUPS = KTOP // SPAN
 BLOCK = 128
+NRHS = 128
 KEEP = 14
 SLOTS = KEEP + 1
 MOVED = {
-    4: ((14, 16, 8, 6),),
-    5: ((14, 16, 8, 2), (16, 20, 12, 6)),
-    6: ((14, 24, 24, 14),),
-    7: ((14, 24, 24, 10), (24, 28, 28, 14)),
+    4: ((14, 16, lambda i: i - 8, 6),),
+    5: ((14, 16, lambda i: i - 8, 2), (16, 20, lambda i: (i - 12) ^ 2, 6)),
+    6: ((14, 24, lambda i: i - 24, 14),),
+    7: ((14, 24, lambda i: i - 24, 10), (24, 28, lambda i: (i - 28) ^ 2, 14)),
 }
 FIRST, SECOND = 10, 4
 
@@ -70,8 +71,8 @@
         if count:
             body = functools.partial(step, d=i, shift=0)
             carry = lax.fori_loop(0, count, body, carry, unroll=unroll)
-        for first, end, back, shift in MOVED.get(g, ()):
-            body = functools.partial(step, d=i - back, shift=shift)
+        for first, end, device, shift in MOVED.get(g, ()):
+            body = functools.partial(step, d=device(i), shift=shift)
             carry = lax.fori_loop(first, end, body, carry, unroll=unroll)
         return carry
 
@@ -135,7 +136,9 @@
 def dot3(left, right):
     (a, b), (c, d) = left, right
     dot = functools.partial(jnp.dot, preferred_element_type=jnp.float32)
-    return dot(a, c) + (dot(a, d) + dot(b, c))
+    both = dot(jnp.concatenate([a, b], axis=0), c)
+    rows = a.shape[0]
+    return both[:rows] + (dot(a, d) + both[rows:])
 
 
 def prepare_kernel(*refs):
@@ -204,14 +207,13 @@
     solved = split(
         jnp.concatenate([columns_of(step * blocks + t) for t in range(blocks)], axis=1)
     )
-    acc[0] += dot3(solved, split(root_panel_ref[...]))
-    for m in range(mids):
-        acc[1 + m] += dot3(solved, split(mid_panel_ref[m]))
+    panels = [root_panel_ref[...]] + [mid_panel_ref[m] for m in range(mids)]
+    acc[...] += dot3(solved, split(jnp.concatenate(panels, axis=1)))
 
     @pl.when(step == pl.num_programs(0) - 1)
     def _():
         top_out[...] = ordered(columns_of(place_ref[0])).T
-        pulls = [ordered(acc[n]).T for n in range(1 + mids)]
+        pulls = [ordered(acc[:, n * BLOCK : (n + 1) * BLOCK]).T for n in range(1 + mids)]
         root = dot3((root_inverse_ref[0, 0], root_inverse_ref[0, 1]), split(forward_root_ref[...] - pulls[0]))
         root_out[...] = root
         root = split(root)
@@ -231,7 +233,7 @@
 
 def finish(place, near, far, root_panel, mid_panel, *small):
     mids, leaves = mid_panel.shape[0], small[2].shape[0]
-    steps = 8
+    steps = 4
     rows = KTOP * BLOCK // steps
 
     def whole(value):
@@ -257,7 +259,7 @@
         ]
         + [whole(value) for value in small],
         out_specs=tuple(whole(value) for value in shapes),
-        scratch_shapes=[pltpu.VMEM((1 + mids, BLOCK, BLOCK), jnp.float32)],
+        scratch_shapes=[pltpu.VMEM((NRHS, (1 + mids) * BLOCK), jnp.float32)],
         compiler_params=pltpu.CompilerParams(vmem_limit_bytes=60 * 2**20),
     )(place, near, far, root_panel, mid_panel, *small)
 
@@ -327,8 +329,8 @@
     )(pattern_row, inverse, factor_row)
     moves = ([], [])
     for g, parts in MOVED.items():
-        for move, (_, _, back, _) in zip(moves, parts):
-            move += [(i, i - back) for i in range(SPAN * g, SPAN * (g + 1))]
+        for move, (_, _, device, _) in zip(moves, parts):
+            move += [(i, device(i)) for i in range(SPAN * g, SPAN * (g + 1))]
     first = lax.ppermute(first, GRID, moves[0])
     second = lax.ppermute(second, GRID, moves[1])
     return pl.pallas_call(merge_kernel, out_shape=out((SLOTS, part, BLOCK)))(

time: 196 us -> 193 us (0.985)
  Pallas kernels: 32 us -> 29.6 us
    pallas_call x1, Pallas kernels: 11.1 us -> 8.64 us  [finish(): pl.pallas_call(finish_kernel, grid=(steps,), out_shape=shapes, in_specs=[...]
where the time goes in v6:
time: 193 us
  blocking collectives  61.5 us (32%)
  waiting for transfers between devices  61.3 us (32%)
  Pallas kernels  29.6 us (15%)
  between operations  14.4 us (7%)
  matrix products  10.8 us (6%)
  starting transfers between devices  6.7 us (3%)
  local copies, waits for them, and re-layouts  4.61 us (2%)
  other arithmetic  4.12 us (2%)
    all_gather x1, waiting for transfers between devices, local(): factor = lax.all_gather(packed, ('layer',) + GRID, axis=0)  46.7 us
    all_to_all x1, blocking collectives, local(): parts = lax.all_to_all(home + swap_cores(away), 'layer', 0, 0, tiled=True)  27.1 us
    all_to_all x1, blocking collectives, local(): near = lax.all_to_all(everywhere, ('layer', 'chip'), 0, 0, tiled=True)  24.3 us
    pallas_call x1, Pallas kernels, sweep(): pl.pallas_call(sweep_kernel, out_shape=jax.ShapeDtypeStruct((KTOP, BLOCK)...  14.1 us
    ppermute x1, waiting for transfers between devices, pack_rows(): second = lax.ppermute(second, GRID, moves[1])  11.2 us
    dot_general x7, matrix products, product(): jnp.einsum(spec, left, right, precision=lax.Precision.HIGHEST, preferred_...  10.8 us
    all_to_all x1, blocking collectives, local(): residual = lax.all_to_all(parts, 'chip', 0, 0, tiled=True).sum(axis=0)  10 us
    pallas_call x1, Pallas kernels, finish(): pl.pallas_call(finish_kernel, grid=(steps,), out_shape=shapes, in_specs=[...  8.64 us
  transfers between devices with their start and end apart: 5, of which 4 were waited for; matrix products, arithmetic and copies ran while one was open for 9% of the time, Pallas kernels for 1%

profile of v6, /device:TPU:1, one launch (start us, length us, event | category | flops | bytes accessed | tf_op | source)
XLA Modules:
  0.0 193.0 jit_solution(2703321666644399656)
XLA Ops:
  7.3 2.8 %shard_map.166 = (f32[15,32,128]{2,1,0:T(8,128)}, f32[10,32,128]{2,1,0:T(8,128)}, f32[4,32,128]{2,1,0:T(8,128)}) custom-call(s32[1,32]{1,0:T(1,128)} %pattern_ref.1, f32[128,128]{1,0:T(8,128)} %bitcast.84, f32[128,4096]{1,0:T(8,128)} %bitcast.76), custom_call_target="tpu_custom_call" | custom-call | tf_op jit(solution)/shard_map/pallas_call | solution.py:310
  10.1 1.4 collective-permute-start.1
  11.5 1.3 collective-permute-start.2
  12.8 11.2 %collective-permute-done.2.second_ref = f32[4,32,128]{2,1,0:T(8,128)S(1)} collective-permute-done((f32[4,32,128]{2,1,0:T(8,128)}, f32[4,32,128]{2,1,0:T(8,128)S(1)}, u32[]{:S(2)}, u32[]{:S(2)}) %collective-permute-start.2) | collective-permute-done | bytes 65568 | tf_op jit(solution)/shard_map/ppermute | solution.py:335
  24.0 0.6 copy-done.15
  24.7 1.8 shard_map.167
  26.5 0.1 copy.31
  26.7 0.4 fusion.2.forward_leaf_ref
  27.2 0.6 bitcast_reduce_fusion
  27.8 0.4 convolution_bitcast_fusion.1.forward_mid_ref
  28.2 0.4 fusion.1
  28.6 0.3 fusion.4
  28.9 6.8 %convolution_bitcast_fusion = f32[128,4096]{1,0:T(8,128)S(1)} fusion(f32[2,128,128]{2,1,0:T(8,128)S(1)} %convolution_bitcast_fusion.1.forward_mid_ref, f32[1,1,2,4096,128]{4,3,2,1,0:T(8,128)} %param.20), kind=kOutput, calls=%fused_computation | convolution fusion | flops 1610612736 | bytes 6422528 | tf_op jit(solution)/shard_map/mbr,mkb->rk/dot_general | solution.py:28
  35.7 2.0 %fusion = f32[16,8,32,128]{3,1,2,0:T(8,128)S(1)} fusion(f32[128,4096]{1,0:T(8,128)S(1)} %convolution_bitcast_fusion, f32[128,128]{1,0:T(8,128)S(1)} %fusion.4, f32[1,1,4096,128]{3,2,1,0:T(8,128)S(1)} %copy-done.1), kind=kOutput, calls=%fused_computation.3 | convolution fusion | flops 805830656 | bytes 6356992 | tf_op jit(solution)/shard_map/br,kb->rk/dot_general | solution.py:28
  37.7 1.7 copy.42
  39.5 2.3 %shard_map.165 = (bf16[1,2,128,128]{3,2,1,0:T(8,128)(2,1)}, bf16[2,2,128,128]{3,2,1,0:T(8,128)(2,1)}, bf16[2,2,128,128]{3,2,1,0:T(8,128)(2,1)}, bf16[4,2,128,128]{3,2,1,0:T(8,128)(2,1)}, bf16[4,2,128,128]{3,2,1,0:T(8,128)(2,1)}) custom-call(f32[1,128,128]{2,1,0:T(8,128)} %bitcast.83, f32[2,128,128]{2,1,0:T(8,128)} %bitcast.81, f32[2,128,128]{2,1,0:T(8,128)} %bitcast.80, ...), custom_call_target="tpu_custom_call" | custom-call | tf_op jit(solution)/shard_map/pallas_call | solution.py:154
  41.8 2.0 %bitcast_subtract_fusion = f32[128,32,128]{2,1,0:T(8,128)S(1)} fusion(f32[16,8,32,128]{3,2,1,0:T(8,128)} %copy.42, f32[128,128]{1,0:T(8,128)S(1)} %copy.36, pred[32]{0:T(512)(128)(4,1)S(1)} %compare_and_fusion), kind=kLoop, calls=%fused_computation.2 | loop fusion | flops 1048576 | bytes 4259872 | tf_op jit(solution)/shard_map/sub | solution.py:388
  43.9 1.9 collective-permute-start
  45.8 2.4 %collective-permute-done = f32[64,32,128]{2,1,0:T(8,128)} collective-permute-done((f32[64,32,128]{2,1,0:T(8,128)S(1)}, f32[64,32,128]{2,1,0:T(8,128)}, u32[]{:S(2)}, u32[]{:S(2)}) %collective-permute-start) | collective-permute-done | bytes 1048608 | tf_op jit(solution)/shard_map/ppermute | solution.py:342
  48.2 1.4 dynamic-slice_add_fusion
  49.6 27.1 %all_to_all.15 = f32[64,32,128]{2,1,0:T(8,128)S(1)} all-to-all(f32[64,32,128]{2,1,0:T(8,128)S(1)} %dynamic-slice_add_fusion), channel_id=1, replica_groups=mesh['layer'=4,'chip'=16,'core'=2] {'layer'}, dimensions={0} | all-to-all | bytes 2097152 | tf_op jit(solution)/shard_map/all_to_all | solution.py:395
  76.9 10.0 %all_to_all.16 = f32[16,32,128]{2,1,0:T(8,128)S(1)} all-to-all(f32[16,32,128]{2,1,0:T(8,128)S(1)} %reduce_sum.28), channel_id=1, replica_groups=mesh['layer'=4,'chip'=16,'core'=2] {'chip'}, dimensions={0} | all-to-all | bytes 524288 | tf_op jit(solution)/shard_map/all_to_all | solution.py:397
  86.9 46.7 %all-gather.3.cloned.1.call-done = f32[1920,32,128]{2,1,0:T(8,128)} async-done(((f32[15,32,128]{2,1,0:T(8,128)}), f32[1920,32,128]{2,1,0:T(8,128)}) %all-gather.3.cloned.1.call-update) | async-done | bytes 31457296 | tf_op jit(solution)/shard_map/all_gather | solution.py:368
  133.7 14.1 %shard_map.168 = f32[32,128]{1,0:T(8,128)S(1)} custom-call(f32[32,128]{1,0:T(8,128)S(1)} %reduce_sum.29.rhs_ref, f32[128,15,32,128]{3,2,1,0:T(8,128)} %bitcast.71), custom_call_target="tpu_custom_call" | custom-call | tf_op jit(solution)/shard_map/pallas_call | solution.py:115
  147.8 0.1 broadcast_in_dim.43
  147.9 24.3 %all_to_all.17 = f32[64,32,128]{2,1,0:T(8,128)S(1)} all-to-all(f32[64,32,128]{2,1,0:T(8,128)S(1)} %broadcast_in_dim.43), channel_id=1, replica_groups=mesh['layer'=4,'chip'=16,'core'=2] {'layer','chip'}, dimensions={0} | all-to-all | bytes 2097152 | tf_op jit(solution)/shard_map/all_to_all | solution.py:401
  172.2 2.0 %collective-permute-start.3 = (f32[64,32,128]{2,1,0:T(8,128)S(1)}, f32[64,32,128]{2,1,0:T(8,128)S(1)}, u32[]{:S(2)}, u32[]{:S(2)}) collective-permute-start(f32[64,32,128]{2,1,0:T(8,128)S(1)} %all_to_all.17), channel_id=1, source_target_pairs={{0,1},{1,0},{2,3},{3,2},{4,5},{5,4},{6,7},{7,6},{8,9},{9,8},{10,11... | collective-permute-start | bytes 3145736 | tf_op jit(solution)/shard_map/ppermute | solution.py:342
  174.2 0.7 copy.37
  174.9 0.6 pad_add_fusion.place_ref
  175.5 1.0 collective-permute-done.3
  176.5 1.0 copy-done.5
  177.5 8.6 %shard_map.169 = (f32[4,128,128]{2,1,0:T(8,128)}, f32[2,128,128]{2,1,0:T(8,128)}, f32[128,128]{1,0:T(8,128)}, f32[128,128]{1,0:T(8,128)}) custom-call(s32[2]{0:T(128)} %pad_add_fusion.place_ref, f32[2048,128]{1,0:T(8,128)} %bitcast.74, f32[2048,128]{1,0:T(8,128)} %bitcast.77, f32[4096,128]{1,0:T(8,128)} %bitcast.73, f32[2,4096,128]{2,1,0:T(8,128)} %bitcast.72, ...), custom_call_target="tpu_custom_call" | custom-call | tf_op jit(solution)/shard_map/pallas_call | solution.py:249
  (39 shorter events, 0.6 us)
Async XLA Ops:
  7.2 19.6 %copy-start = (f32[1,1,4,128,128]{4,3,2,1,0:T(8,128)S(1)}, f32[1,1,4,128,128]{4,3,2,1,0:T(8,128)}, u32[]{:S(2)}) copy-start(f32[1,1,4,128,128]{4,3,2,1,0:T(8,128)} %param.16) | copy-start | bytes 786436
  7.2 19.3 %copy-start.12 = (f32[1,1,2,128,128]{4,3,2,1,0:T(8,128)S(1)}, f32[1,1,2,128,128]{4,3,2,1,0:T(8,128)}, u32[]{:S(2)}) copy-start(f32[1,1,2,128,128]{4,3,2,1,0:T(8,128)} %param.19) | copy-start | bytes 393220
  7.2 19.4 %copy-start.13 = (f32[1,1,128,128]{3,2,1,0:T(8,128)S(1)}, f32[1,1,128,128]{3,2,1,0:T(8,128)}, u32[]{:S(2)}) copy-start(f32[1,1,128,128]{3,2,1,0:T(8,128)} %param.23) | copy-start | bytes 196612
  7.2 19.5 %copy-start.6 = (f32[1,1,4,128,128]{4,3,2,1,0:T(8,128)S(1)}, f32[1,1,4,128,128]{4,3,2,1,0:T(8,128)}, u32[]{:S(2)}) copy-start(f32[1,1,4,128,128]{4,3,2,1,0:T(8,128)} %param.14) | copy-start | bytes 786436
  7.2 126.5 %all-gather.3.cloned.1.call-start = ((), (), s32[]{:S(2)}) async-start(), calls=%async_computation.3 | async-start | bytes 31703040 | tf_op jit(solution)/shard_map/all_gather | solution.py:368
  7.3 19.9 %copy-start.7 = (f32[1,1,4,128,128]{4,3,2,1,0:T(8,128)S(1)}, f32[1,1,4,128,128]{4,3,2,1,0:T(8,128)}, u32[]{:S(2)}) copy-start(f32[1,1,4,128,128]{4,3,2,1,0:T(8,128)} %param.15) | copy-start | bytes 786436
  7.3 20.5 %copy-start.9 = (f32[1,1,2,128,128]{4,3,2,1,0:T(8,128)S(1)}, f32[1,1,2,128,128]{4,3,2,1,0:T(8,128)}, u32[]{:S(2)}) copy-start(f32[1,1,2,128,128]{4,3,2,1,0:T(8,128)} %param.17) | copy-start | bytes 393220
  10.1 18.1 %copy-start.8 = (f32[1,1,2,128,128]{4,3,2,1,0:T(8,128)S(1)}, f32[1,1,2,128,128]{4,3,2,1,0:T(8,128)}, u32[]{:S(2)}) copy-start(f32[1,1,2,128,128]{4,3,2,1,0:T(8,128)} %param.18) | copy-start | bytes 393220
  10.1 18.5 %copy-start.10 = (f32[1,1,128,128]{3,2,1,0:T(8,128)S(1)}, f32[1,1,128,128]{3,2,1,0:T(8,128)}, u32[]{:S(2)}) copy-start(f32[1,1,128,128]{3,2,1,0:T(8,128)} %param.21) | copy-start | bytes 196612
  10.1 13.9 %collective-permute-start.1 = (f32[10,32,128]{2,1,0:T(8,128)}, f32[10,32,128]{2,1,0:T(8,128)S(1)}, u32[]{:S(2)}, u32[]{:S(2)}) collective-permute-start(f32[10,32,128]{2,1,0:T(8,128)} %get-tuple-element.29), channel_id=1, source_target_pairs={{16,8},{17,9},{18,10},{19,11},{20,12},{21,13},{22,14},{23,15},{24,... | collective-permute-start | bytes 491528 | tf_op jit(solution)/shard_map/ppermute | solution.py:334
  11.5 12.5 %collective-permute-start.2 = (f32[4,32,128]{2,1,0:T(8,128)}, f32[4,32,128]{2,1,0:T(8,128)S(1)}, u32[]{:S(2)}, u32[]{:S(2)}) collective-permute-start(f32[4,32,128]{2,1,0:T(8,128)} %get-tuple-element.30), channel_id=1, source_target_pairs={{20,10},{21,11},{22,8},{23,9},{28,2},{29,3},{30,0},{31,1},{52,42},... | collective-permute-start | bytes 196616 | tf_op jit(solution)/shard_map/ppermute | solution.py:335
  24.0 0.6 copy-start.15
  24.0 0.7 copy-start.11
  27.2 8.6 %copy-start.3 = (f32[4,128,128]{2,1,0:T(8,128)}, f32[4,128,128]{2,1,0:T(8,128)S(1)}, u32[]{:S(2)}) copy-start(f32[4,128,128]{2,1,0:T(8,128)S(1)} %fusion.2.forward_leaf_ref) | copy-start | bytes 786436
  28.2 7.5 %copy-start.4 = (f32[2,128,128]{2,1,0:T(8,128)}, f32[2,128,128]{2,1,0:T(8,128)S(1)}, u32[]{:S(2)}) copy-start(f32[2,128,128]{2,1,0:T(8,128)S(1)} %convolution_bitcast_fusion.1.forward_mid_ref) | copy-start | bytes 393220
  28.9 6.9 %copy-start.1 = (f32[1,1,4096,128]{3,2,1,0:T(8,128)S(1)}, f32[1,1,4096,128]{3,2,1,0:T(8,128)}, u32[]{:S(2)}) copy-start(f32[1,1,4096,128]{3,2,1,0:T(8,128)} %param.22) | copy-start | bytes 6291460
  37.7 1.7 copy-start.14
  43.9 4.3 %collective-permute-start = (f32[64,32,128]{2,1,0:T(8,128)S(1)}, f32[64,32,128]{2,1,0:T(8,128)}, u32[]{:S(2)}, u32[]{:S(2)}) collective-permute-start(f32[64,32,128]{2,1,0:T(8,128)S(1)} %constant_dynamic-slice_fusion), channel_id=1, source_target_pairs={{0,1},{1,0},{2,3},{3,2},{4,5},{5,4},{6,7},{7,6},{8,9},{9,8},{10,11... | collective-permute-start | bytes 3145736 | tf_op jit(solution)/shard_map/ppermute | solution.py:342
  172.2 4.3 %copy-start.2 = (f32[64,32,128]{2,1,0:T(8,128)}, f32[64,32,128]{2,1,0:T(8,128)S(1)}, u32[]{:S(2)}) copy-start(f32[64,32,128]{2,1,0:T(8,128)S(1)} %all_to_all.17) | copy-start | bytes 3145732
  172.2 4.3 %collective-permute-start.3 = (f32[64,32,128]{2,1,0:T(8,128)S(1)}, f32[64,32,128]{2,1,0:T(8,128)S(1)}, u32[]{:S(2)}, u32[]{:S(2)}) collective-permute-start(f32[64,32,128]{2,1,0:T(8,128)S(1)} %all_to_all.17), channel_id=1, source_target_pairs={{0,1},{1,0},{2,3},{3,2},{4,5},{5,4},{6,7},{7,6},{8,9},{9,8},{10,11... | collective-permute-start | bytes 3145736 | tf_op jit(solution)/shard_map/ppermute | solution.py:342
  176.5 1.0 copy-start.5
Sparse Core Ops, SparseCore 0:
  26.6 107.0 all-gather.2

commit v7 on v6

--- a/solution.py
+++ b/solution.py
@@ -233,7 +233,7 @@
 
 def finish(place, near, far, root_panel, mid_panel, *small):
     mids, leaves = mid_panel.shape[0], small[2].shape[0]
-    steps = 4
+    steps = 2
     rows = KTOP * BLOCK // steps
 
     def whole(value):
@@ -290,16 +290,27 @@
         second_ref[t] = weighted(start + t)
 
 
-def merge_kernel(keep_ref, first_ref, second_ref, out_ref):
+def merge_kernel(keep_hbm, first_ref, second_ref, out_hbm, sems):
     own_group = (lax.axis_index("chip") * 2 + lax.axis_index("core")) // SPAN
-    own = SPAN * own_group
-    out_ref[KEEP] = keep_ref[KEEP]
-    for slot in range(KEEP):
-        got = first_ref[jnp.clip(slot - own, 0, FIRST - 1)]
-        if slot >= KEEP - SECOND:
-            late = own_group % 2 == 0
-            got = jnp.where(late, second_ref[slot - (KEEP - SECOND)], got)
-        out_ref[slot] = jnp.where(slot < own, keep_ref[slot], got)
+    for g in range(GROUPS // 2):
+        second = SECOND if g % 2 == 0 else 0
+        own, end = SPAN * g, KEEP - second
+
+        @pl.when(own_group == g)
+        def _():
+            copies = [
+                pltpu.make_async_copy(
+                    first_ref.at[pl.ds(0, end - own)], out_hbm.at[pl.ds(own, end - own)], sems.at[0]
+                )
+            ]
+            if second:
+                copies.append(
+                    pltpu.make_async_copy(second_ref, out_hbm.at[pl.ds(end, second)], sems.at[1])
+                )
+            for copy in copies:
+                copy.start()
+            for copy in copies:
+                copy.wait()
 
 
 def pack_rows(factor_row, pattern_row, inverse, layers):
@@ -333,9 +344,15 @@
             move += [(i, device(i)) for i in range(SPAN * g, SPAN * (g + 1))]
     first = lax.ppermute(first, GRID, moves[0])
     second = lax.ppermute(second, GRID, moves[1])
-    return pl.pallas_call(merge_kernel, out_shape=out((SLOTS, part, BLOCK)))(
-        keep, first, second
-    )
+    anywhere = pl.BlockSpec(memory_space=pl.ANY)
+    return pl.pallas_call(
+        merge_kernel,
+        out_shape=out((SLOTS, part, BLOCK)),
+        in_specs=[anywhere] + [vmem] * 2,
+        out_specs=anywhere,
+        scratch_shapes=[pltpu.SemaphoreType.DMA((2,))],
+        input_output_aliases={0: 0},
+    )(keep, first, second)
 
 
 def swap_cores(value):

time: 193 us -> 193 us (level)
  no operation moved by 1% of the time
where the time goes in v7:
time: 193 us; the launch traced here: 192 us
  blocking collectives  61.5 us (32%)
  waiting for transfers between devices  61.3 us (32%)
  Pallas kernels  28.8 us (15%)
  between operations  14.4 us (7%)
  matrix products  10.8 us (6%)
  starting transfers between devices  6.69 us (3%)
  local copies, waits for them, and re-layouts  4.61 us (2%)
  other arithmetic  4.19 us (2%)
    all_gather x1, waiting for transfers between devices, local(): factor = lax.all_gather(packed, ('layer',) + GRID, axis=0)  46.7 us
    all_to_all x1, blocking collectives, local(): parts = lax.all_to_all(home + swap_cores(away), 'layer', 0, 0, tiled=True)  27.1 us
    all_to_all x1, blocking collectives, local(): near = lax.all_to_all(everywhere, ('layer', 'chip'), 0, 0, tiled=True)  24.3 us
    pallas_call x1, Pallas kernels, sweep(): pl.pallas_call(sweep_kernel, out_shape=jax.ShapeDtypeStruct((KTOP, BLOCK)...  14.1 us
    ppermute x1, waiting for transfers between devices, pack_rows(): second = lax.ppermute(second, GRID, moves[1])  11.2 us
    dot_general x7, matrix products, product(): jnp.einsum(spec, left, right, precision=lax.Precision.HIGHEST, preferred_...  10.8 us
    all_to_all x1, blocking collectives, local(): residual = lax.all_to_all(parts, 'chip', 0, 0, tiled=True).sum(axis=0)  10 us
    pallas_call x1, Pallas kernels, finish(): pl.pallas_call(finish_kernel, grid=(steps,), out_shape=shapes, in_specs=[...  8.01 us
  transfers between devices with their start and end apart: 5, of which 4 were waited for; matrix products, arithmetic and copies ran while one was open for 9% of the time, Pallas kernels for 1%

profile of v7, /device:TPU:1, one launch (start us, length us, event | category | flops | bytes accessed | tf_op | source)
XLA Modules:
  0.0 192.2 jit_solution(8178882519016312374)
XLA Ops:
  7.3 2.8 %shard_map.166 = (f32[15,32,128]{2,1,0:T(8,128)}, f32[10,32,128]{2,1,0:T(8,128)}, f32[4,32,128]{2,1,0:T(8,128)}) custom-call(s32[1,32]{1,0:T(1,128)} %pattern_ref.1, f32[128,128]{1,0:T(8,128)} %bitcast.84, f32[128,4096]{1,0:T(8,128)} %bitcast.76), custom_call_target="tpu_custom_call" | custom-call | tf_op jit(solution)/shard_map/pallas_call | solution.py:321
  10.1 1.4 collective-permute-start.1
  11.5 1.3 collective-permute-start.2
  12.8 11.2 %collective-permute-done.2.second_ref = f32[4,32,128]{2,1,0:T(8,128)S(1)} collective-permute-done((f32[4,32,128]{2,1,0:T(8,128)}, f32[4,32,128]{2,1,0:T(8,128)S(1)}, u32[]{:S(2)}, u32[]{:S(2)}) %collective-permute-start.2) | collective-permute-done | bytes 65568 | tf_op jit(solution)/shard_map/ppermute | solution.py:346
  24.0 0.6 copy-done.15
  24.7 1.6 shard_map.167
  26.4 0.1 copy.32
  26.6 0.4 fusion.2.forward_leaf_ref
  27.0 0.6 bitcast_reduce_fusion
  27.6 0.4 convolution_bitcast_fusion.1.forward_mid_ref
  28.1 0.4 fusion.1
  28.5 0.3 fusion.4
  28.7 6.8 %convolution_bitcast_fusion = f32[128,4096]{1,0:T(8,128)S(1)} fusion(f32[2,128,128]{2,1,0:T(8,128)S(1)} %convolution_bitcast_fusion.1.forward_mid_ref, f32[1,1,2,4096,128]{4,3,2,1,0:T(8,128)} %param.20), kind=kOutput, calls=%fused_computation | convolution fusion | flops 1610612736 | bytes 6422528 | tf_op jit(solution)/shard_map/mbr,mkb->rk/dot_general | solution.py:28
  35.6 2.0 %fusion = f32[16,8,32,128]{3,1,2,0:T(8,128)S(1)} fusion(f32[128,4096]{1,0:T(8,128)S(1)} %convolution_bitcast_fusion, f32[128,128]{1,0:T(8,128)S(1)} %fusion.4, f32[1,1,4096,128]{3,2,1,0:T(8,128)S(1)} %copy-done.1), kind=kOutput, calls=%fused_computation.3 | convolution fusion | flops 805830656 | bytes 6356992 | tf_op jit(solution)/shard_map/br,kb->rk/dot_general | solution.py:28
  37.6 1.7 copy.43
  39.4 2.3 %shard_map.165 = (bf16[1,2,128,128]{3,2,1,0:T(8,128)(2,1)}, bf16[2,2,128,128]{3,2,1,0:T(8,128)(2,1)}, bf16[2,2,128,128]{3,2,1,0:T(8,128)(2,1)}, bf16[4,2,128,128]{3,2,1,0:T(8,128)(2,1)}, bf16[4,2,128,128]{3,2,1,0:T(8,128)(2,1)}) custom-call(f32[1,128,128]{2,1,0:T(8,128)} %bitcast.83, f32[2,128,128]{2,1,0:T(8,128)} %bitcast.81, f32[2,128,128]{2,1,0:T(8,128)} %bitcast.80, ...), custom_call_target="tpu_custom_call" | custom-call | tf_op jit(solution)/shard_map/pallas_call | solution.py:154
  41.7 2.0 %bitcast_subtract_fusion = f32[128,32,128]{2,1,0:T(8,128)S(1)} fusion(f32[16,8,32,128]{3,2,1,0:T(8,128)} %copy.43, f32[128,128]{1,0:T(8,128)S(1)} %copy.37, pred[32]{0:T(512)(128)(4,1)S(1)} %compare_and_fusion), kind=kLoop, calls=%fused_computation.2 | loop fusion | flops 1048576 | bytes 4259872 | tf_op jit(solution)/shard_map/sub | solution.py:405
  43.7 1.9 collective-permute-start
  45.7 2.4 %collective-permute-done = f32[64,32,128]{2,1,0:T(8,128)} collective-permute-done((f32[64,32,128]{2,1,0:T(8,128)S(1)}, f32[64,32,128]{2,1,0:T(8,128)}, u32[]{:S(2)}, u32[]{:S(2)}) %collective-permute-start) | collective-permute-done | bytes 1048608 | tf_op jit(solution)/shard_map/ppermute | solution.py:359
  48.1 1.4 dynamic-slice_add_fusion
  49.5 27.1 %all_to_all.15 = f32[64,32,128]{2,1,0:T(8,128)S(1)} all-to-all(f32[64,32,128]{2,1,0:T(8,128)S(1)} %dynamic-slice_add_fusion), channel_id=1, replica_groups=mesh['layer'=4,'chip'=16,'core'=2] {'layer'}, dimensions={0} | all-to-all | bytes 2097152 | tf_op jit(solution)/shard_map/all_to_all | solution.py:412
  76.7 10.0 %all_to_all.16 = f32[16,32,128]{2,1,0:T(8,128)S(1)} all-to-all(f32[16,32,128]{2,1,0:T(8,128)S(1)} %reduce_sum.28), channel_id=1, replica_groups=mesh['layer'=4,'chip'=16,'core'=2] {'chip'}, dimensions={0} | all-to-all | bytes 524288 | tf_op jit(solution)/shard_map/all_to_all | solution.py:414
  86.8 46.7 %all-gather.3.cloned.1.call-done = f32[1920,32,128]{2,1,0:T(8,128)} async-done(((f32[15,32,128]{2,1,0:T(8,128)}), f32[1920,32,128]{2,1,0:T(8,128)}) %all-gather.3.cloned.1.call-update) | async-done | bytes 31457296 | tf_op jit(solution)/shard_map/all_gather | solution.py:385
  133.5 14.1 %shard_map.168 = f32[32,128]{1,0:T(8,128)S(1)} custom-call(f32[32,128]{1,0:T(8,128)S(1)} %reduce_sum.29.rhs_ref, f32[128,15,32,128]{3,2,1,0:T(8,128)} %bitcast.71), custom_call_target="tpu_custom_call" | custom-call | tf_op jit(solution)/shard_map/pallas_call | solution.py:115
  147.7 0.1 broadcast_in_dim.43
  147.8 24.3 %all_to_all.17 = f32[64,32,128]{2,1,0:T(8,128)S(1)} all-to-all(f32[64,32,128]{2,1,0:T(8,128)S(1)} %broadcast_in_dim.43), channel_id=1, replica_groups=mesh['layer'=4,'chip'=16,'core'=2] {'layer','chip'}, dimensions={0} | all-to-all | bytes 2097152 | tf_op jit(solution)/shard_map/all_to_all | solution.py:418
  172.1 2.0 %collective-permute-start.3 = (f32[64,32,128]{2,1,0:T(8,128)S(1)}, f32[64,32,128]{2,1,0:T(8,128)S(1)}, u32[]{:S(2)}, u32[]{:S(2)}) collective-permute-start(f32[64,32,128]{2,1,0:T(8,128)S(1)} %all_to_all.17), channel_id=1, source_target_pairs={{0,1},{1,0},{2,3},{3,2},{4,5},{5,4},{6,7},{7,6},{8,9},{9,8},{10,11... | collective-permute-start | bytes 3145736 | tf_op jit(solution)/shard_map/ppermute | solution.py:359
  174.1 0.7 copy.38
  174.8 0.6 pad_add_fusion.place_ref
  175.5 0.9 collective-permute-done.3
  176.4 1.0 copy-done.5
  177.4 8.0 %shard_map.169 = (f32[4,128,128]{2,1,0:T(8,128)}, f32[2,128,128]{2,1,0:T(8,128)}, f32[128,128]{1,0:T(8,128)}, f32[128,128]{1,0:T(8,128)}) custom-call(s32[2]{0:T(128)} %pad_add_fusion.place_ref, f32[2048,128]{1,0:T(8,128)} %bitcast.74, f32[2048,128]{1,0:T(8,128)} %bitcast.77, f32[4096,128]{1,0:T(8,128)} %bitcast.73, f32[2,4096,128]{2,1,0:T(8,128)} %bitcast.72, ...), custom_call_target="tpu_custom_call" | custom-call | tf_op jit(solution)/shard_map/pallas_call | solution.py:249
  (39 shorter events, 0.6 us)
Async XLA Ops:
  7.2 19.4 %copy-start = (f32[1,1,4,128,128]{4,3,2,1,0:T(8,128)S(1)}, f32[1,1,4,128,128]{4,3,2,1,0:T(8,128)}, u32[]{:S(2)}) copy-start(f32[1,1,4,128,128]{4,3,2,1,0:T(8,128)} %param.16) | copy-start | bytes 786436
  7.2 19.2 %copy-start.12 = (f32[1,1,2,128,128]{4,3,2,1,0:T(8,128)S(1)}, f32[1,1,2,128,128]{4,3,2,1,0:T(8,128)}, u32[]{:S(2)}) copy-start(f32[1,1,2,128,128]{4,3,2,1,0:T(8,128)} %param.19) | copy-start | bytes 393220
  7.2 19.3 %copy-start.13 = (f32[1,1,128,128]{3,2,1,0:T(8,128)S(1)}, f32[1,1,128,128]{3,2,1,0:T(8,128)}, u32[]{:S(2)}) copy-start(f32[1,1,128,128]{3,2,1,0:T(8,128)} %param.23) | copy-start | bytes 196612
  7.2 19.4 %copy-start.6 = (f32[1,1,4,128,128]{4,3,2,1,0:T(8,128)S(1)}, f32[1,1,4,128,128]{4,3,2,1,0:T(8,128)}, u32[]{:S(2)}) copy-start(f32[1,1,4,128,128]{4,3,2,1,0:T(8,128)} %param.14) | copy-start | bytes 786436
  7.2 126.3 %all-gather.3.cloned.1.call-start = ((), (), s32[]{:S(2)}) async-start(), calls=%async_computation.3 | async-start | bytes 31703040 | tf_op jit(solution)/shard_map/all_gather | solution.py:385
  7.3 19.8 %copy-start.7 = (f32[1,1,4,128,128]{4,3,2,1,0:T(8,128)S(1)}, f32[1,1,4,128,128]{4,3,2,1,0:T(8,128)}, u32[]{:S(2)}) copy-start(f32[1,1,4,128,128]{4,3,2,1,0:T(8,128)} %param.15) | copy-start | bytes 786436
  7.3 20.4 %copy-start.9 = (f32[1,1,2,128,128]{4,3,2,1,0:T(8,128)S(1)}, f32[1,1,2,128,128]{4,3,2,1,0:T(8,128)}, u32[]{:S(2)}) copy-start(f32[1,1,2,128,128]{4,3,2,1,0:T(8,128)} %param.17) | copy-start | bytes 393220
  10.1 18.0 %copy-start.8 = (f32[1,1,2,128,128]{4,3,2,1,0:T(8,128)S(1)}, f32[1,1,2,128,128]{4,3,2,1,0:T(8,128)}, u32[]{:S(2)}) copy-start(f32[1,1,2,128,128]{4,3,2,1,0:T(8,128)} %param.18) | copy-start | bytes 393220
  10.1 18.4 %copy-start.10 = (f32[1,1,128,128]{3,2,1,0:T(8,128)S(1)}, f32[1,1,128,128]{3,2,1,0:T(8,128)}, u32[]{:S(2)}) copy-start(f32[1,1,128,128]{3,2,1,0:T(8,128)} %param.21) | copy-start | bytes 196612
  10.1 13.9 %collective-permute-start.1 = (f32[10,32,128]{2,1,0:T(8,128)}, f32[10,32,128]{2,1,0:T(8,128)S(1)}, u32[]{:S(2)}, u32[]{:S(2)}) collective-permute-start(f32[10,32,128]{2,1,0:T(8,128)} %get-tuple-element.29), channel_id=1, source_target_pairs={{16,8},{17,9},{18,10},{19,11},{20,12},{21,13},{22,14},{23,15},{24,... | collective-permute-start | bytes 491528 | tf_op jit(solution)/shard_map/ppermute | solution.py:345
  11.5 12.5 %collective-permute-start.2 = (f32[4,32,128]{2,1,0:T(8,128)}, f32[4,32,128]{2,1,0:T(8,128)S(1)}, u32[]{:S(2)}, u32[]{:S(2)}) collective-permute-start(f32[4,32,128]{2,1,0:T(8,128)} %get-tuple-element.30), channel_id=1, source_target_pairs={{20,10},{21,11},{22,8},{23,9},{28,2},{29,3},{30,0},{31,1},{52,42},... | collective-permute-start | bytes 196616 | tf_op jit(solution)/shard_map/ppermute | solution.py:346
  24.0 0.6 copy-start.15
  24.0 0.7 copy-start.11
  27.0 8.6 %copy-start.3 = (f32[4,128,128]{2,1,0:T(8,128)}, f32[4,128,128]{2,1,0:T(8,128)S(1)}, u32[]{:S(2)}) copy-start(f32[4,128,128]{2,1,0:T(8,128)S(1)} %fusion.2.forward_leaf_ref) | copy-start | bytes 786436
  28.1 7.5 %copy-start.4 = (f32[2,128,128]{2,1,0:T(8,128)}, f32[2,128,128]{2,1,0:T(8,128)S(1)}, u32[]{:S(2)}) copy-start(f32[2,128,128]{2,1,0:T(8,128)S(1)} %convolution_bitcast_fusion.1.forward_mid_ref) | copy-start | bytes 393220
  28.7 6.9 %copy-start.1 = (f32[1,1,4096,128]{3,2,1,0:T(8,128)S(1)}, f32[1,1,4096,128]{3,2,1,0:T(8,128)}, u32[]{:S(2)}) copy-start(f32[1,1,4096,128]{3,2,1,0:T(8,128)} %param.22) | copy-start | bytes 6291460
  37.6 1.7 copy-start.14
  43.7 4.3 %collective-permute-start = (f32[64,32,128]{2,1,0:T(8,128)S(1)}, f32[64,32,128]{2,1,0:T(8,128)}, u32[]{:S(2)}, u32[]{:S(2)}) collective-permute-start(f32[64,32,128]{2,1,0:T(8,128)S(1)} %constant_dynamic-slice_fusion), channel_id=1, source_target_pairs={{0,1},{1,0},{2,3},{3,2},{4,5},{5,4},{6,7},{7,6},{8,9},{9,8},{10,11... | collective-permute-start | bytes 3145736 | tf_op jit(solution)/shard_map/ppermute | solution.py:359
  172.1 4.3 %copy-start.2 = (f32[64,32,128]{2,1,0:T(8,128)}, f32[64,32,128]{2,1,0:T(8,128)S(1)}, u32[]{:S(2)}) copy-start(f32[64,32,128]{2,1,0:T(8,128)S(1)} %all_to_all.17) | copy-start | bytes 3145732
  172.1 4.3 %collective-permute-start.3 = (f32[64,32,128]{2,1,0:T(8,128)S(1)}, f32[64,32,128]{2,1,0:T(8,128)S(1)}, u32[]{:S(2)}, u32[]{:S(2)}) collective-permute-start(f32[64,32,128]{2,1,0:T(8,128)S(1)} %all_to_all.17), channel_id=1, source_target_pairs={{0,1},{1,0},{2,3},{3,2},{4,5},{5,4},{6,7},{7,6},{8,9},{9,8},{10,11... | collective-permute-start | bytes 3145736 | tf_op jit(solution)/shard_map/ppermute | solution.py:359
  176.4 1.0 copy-start.5
Sparse Core Ops, SparseCore 0:
  26.5 107.0 all-gather.2
